TPU v7x, 512 devices: a whole 4x4x16 slice. The times are simulated.
512 devices in a mesh: dp: 2 (over core), expert: 16 (over x, y), tensor: 16 (over z).
Axes of the slice: x: 4, y: 4, z: 16, core: 2. Of those that a mesh axis runs over, the one named last changes fastest.
Arguments:
- out_grad: bfloat16 [4096, 4096], P(('dp', 'expert', 'tensor')), may hold values from -1.5 to 1.5
- routing: int32 [4096, 2], P(('dp', 'expert')), may hold values from 0 to 15, all different within a row; in each aligned block of 128 rows (0 to 127, 128 to 255, ...) at most 32 rows name the same one
- gate_codes: int32 [4096, 2], P(('dp', 'expert')), may hold values from 16 to 255
- hidden_saved: bfloat16 [2, 16, 16, 32, 12288], P('dp', 'expert', None, None, 'tensor'), may hold values from -6 to 6
- down_weight: bfloat16 [16, 12288, 4096], P('expert', 'tensor', 'dp'), may hold values from -0.0546875 to 0.0546875
- channel_scale: bfloat16 [16, 4096], P('expert', 'dp'), may hold values from 0.0029907227 to 0.029907227
Outputs:
- hidden_grad: bfloat16 [2, 16, 16, 32, 12288], P('dp', 'expert', None, None, 'tensor')
- scale_grad: float32 [16, 4096], P('expert', 'dp')
- gate_grad: float32 [4096, 2], P(('dp', 'expert', 'tensor'))
Inputs may be any that keep to these rules, and one draw needn't show every extreme that they name: `routing`: each token names two different experts; in each aligned block of 128 tokens no expert is named by more than 32 routes; some block reaches 32.
All inputs are finite; a program needn't handle non-finite values.
Results may differ from a plain program's by a relative error of at most 0.0049.
Values may be sent and summed in bfloat16 or wider, within the bound.
A program may use at most 128 MiB of HBM per device.

v0:
```python
import jax
import jax.numpy as jnp
from jax import lax
from jax.sharding import PartitionSpec as P


def slot_places(routing, experts, capacity):
    pair_expert = routing.reshape(-1)
    onehot = (pair_expert[:, None] == jnp.arange(experts, dtype=jnp.int32)[None, :]).astype(
        jnp.int32
    )
    before = jnp.cumsum(onehot, axis=0) - onehot
    return pair_expert * capacity + jnp.sum(before * onehot, axis=1)


def on_device(out_grad, routing, gate_codes, hidden_saved, down_weight, channel_scale):
    experts = lax.axis_size("expert")
    sources = hidden_saved.shape[2]
    capacity = hidden_saved.shape[3]
    unit_width = hidden_saved.shape[4]
    full_width = out_grad.shape[1]
    half_width = down_weight.shape[2]
    slot_index = slot_places(routing, experts, capacity)
    pair_count = slot_index.shape[0]
    slot_owner = (
        jnp.full((experts * capacity,), -1, jnp.int32)
        .at[slot_index]
        .set(jnp.arange(pair_count, dtype=jnp.int32))
    )
    slot_live = slot_owner >= 0
    safe_owner = jnp.maximum(slot_owner, 0)
    token_slot = safe_owner // 2
    gate_slot = jnp.where(
        slot_live, gate_codes.reshape(-1)[safe_owner].astype(jnp.float32) / 256.0, 0.0
    )
    gate_slot = gate_slot.astype(jnp.bfloat16).reshape(experts, capacity)
    whole_rows = lax.all_gather(out_grad, "tensor", axis=0, tiled=True)
    picked = jnp.where(slot_live[:, None], whole_rows[token_slot], jnp.zeros((), jnp.bfloat16))
    arrived, gate_recv = (
        lax.all_to_all(
            picked.reshape(experts, capacity, full_width),
            "expert",
            split_axis=0,
            concat_axis=0,
            tiled=True,
        ),
        lax.all_to_all(gate_slot, "expert", split_axis=0, concat_axis=0, tiled=True),
    )
    slot_rows = arrived.reshape(sources * capacity, full_width)
    gate_rows = gate_recv.reshape(-1).astype(jnp.float32)
    scaled = (gate_rows[:, None] * slot_rows).astype(jnp.bfloat16)
    saved_rows = hidden_saved.reshape(sources * capacity, unit_width)
    weight_piece = lax.all_gather(down_weight, "dp", axis=2, tiled=True)
    scale_piece = lax.all_gather(channel_scale.reshape(1, 1, half_width), "dp", axis=2, tiled=True)
    scale_wide = scale_piece[0].astype(jnp.float32)
    ratio_values = weight_piece[0].astype(jnp.float32) / scale_wide
    bent_ratio = jnp.tanh(ratio_values)
    quantized = (scale_wide * bent_ratio).astype(jnp.bfloat16)
    slope_values = bent_ratio - ratio_values * (1.0 - bent_ratio * bent_ratio)
    raw_grad = lax.dot_general(
        slot_rows, quantized, (((1,), (1,)), ((), ())), preferred_element_type=jnp.float32
    )
    weight_grad = lax.dot_general(
        saved_rows, scaled, (((0,), (0,)), ((), ())), preferred_element_type=jnp.float32
    )
    channel_terms = jnp.sum(weight_grad * slope_values, axis=0)
    scale_part = channel_terms
    raw_grad, scale_part = (raw_grad, scale_part)
    hidden_grad = (gate_rows[:, None] * raw_grad).astype(jnp.bfloat16).reshape(hidden_saved.shape)
    gate_part = jnp.sum(saved_rows.astype(jnp.float32) * raw_grad, axis=1).reshape(
        sources, capacity
    )
    returned = lax.all_to_all(gate_part, "expert", split_axis=0, concat_axis=0, tiled=True)
    pair_values = returned.reshape(-1)[slot_index].reshape(-1, 2)
    gate_grad = lax.psum_scatter(pair_values, "tensor", scatter_dimension=0, tiled=True)
    own_half = lax.psum_scatter(scale_part, "dp", scatter_dimension=0, tiled=True)
    scale_grad = lax.psum(own_half, "tensor")
    return (hidden_grad, scale_grad.reshape(1, half_width), gate_grad)


def solution(mesh):
    in_specs = (
        P(("dp", "expert", "tensor"), None),
        P(("dp", "expert"), None),
        P(("dp", "expert"), None),
        P("dp", "expert", None, None, "tensor"),
        P("expert", "tensor", "dp"),
        P("expert", "dp"),
    )
    out_specs = (
        P("dp", "expert", None, None, "tensor"),
        P("expert", "dp"),
        P(("dp", "expert", "tensor"), None),
    )
    return jax.shard_map(
        on_device, mesh=mesh, in_specs=in_specs, out_specs=out_specs, check_vma=False
    )
```

profile of v0, /device:TPU:6, one launch (start us, length us, event | category | flops | bytes accessed | tf_op | source)
XLA Modules:
  0.0 253.1 jit_solution(15979664332182909704)
XLA Ops:
  7.2 0.0 all-gather.4.cloned.1.call-start
  7.2 0.7 all-gather.4.cloned.1.call-update
  7.9 0.0 all-gather.6.cloned.1.call-start
  7.9 0.7 all-gather.6.cloned.1.call-update
  8.6 0.7 broadcast_multiply_fusion
  9.3 0.8 copy.22
  10.1 0.1 eq.25
  10.3 0.1 eq.29
  10.4 0.8 copy.25
  11.2 0.1 reshape.136
  11.3 0.1 copy.21
  11.4 0.1 mul.61
  11.6 0.6 reduce-window.6
  12.2 0.2 slice_reduce_fusion
  12.4 0.1 fusion.10
  12.5 1.4 scatter_custom_fusion
  14.0 3.5 %gather_fusion = s32[512]{0:T(512)S(1)} fusion(s32[256]{0:T(256)S(1)} %reshape.136, s32[1024]{0:T(1024)S(1)} %pad_clamp_fusion.2), kind=kCustom, calls=%fused_computation | custom fusion | bytes 6144 | tf_op jit(solution)/shard_map/gather | solution.py:34
  17.5 0.7 all_to_all.20
  18.2 9.2 %all-to-all-start = ((bf16[16,1,32]{2,1,0:T(2,128)(2,1)}), bf16[16,1,32]{2,1,0:T(2,128)(2,1)S(1)}, u32[]{:S(2)}, u32[]{:S(2)}) async-start(bf16[16,1,32]{2,1,0:T(2,128)(2,1)} %all_to_all.20), calls=%async_computation | async-start | bytes 16384 | tf_op jit(solution)/shard_map/all_to_all | solution.py:47
  27.4 0.1 broadcast_in_dim.36
  27.4 58.1 %all-gather.4.cloned.1.call-done = bf16[128,4096]{1,0:T(8,128)(2,1)} async-done(((bf16[8,4096]{1,0:T(8,128)(2,1)}), bf16[128,4096]{1,0:T(8,128)(2,1)}) %all-gather.4.cloned.1.call-update) | async-done | bytes 1048592 | tf_op jit(solution)/shard_map/all_gather | solution.py:37
  85.5 10.0 %gather_fusion.1 = bf16[512,4096]{1,0:T(8,128)(2,1)} fusion(bf16[128,4096]{1,0:T(8,128)(2,1)} %all-gather.4.cloned.1.call-done, s32[1024]{0:T(1024)S(1)} %pad_clamp_fusion.1), kind=kCustom, calls=%fused_computation.1 | custom fusion | bytes 8390656 | tf_op jit(solution)/shard_map/gather | solution.py:38
  95.5 4.6 %broadcast_select_fusion = bf16[16,32,4096]{2,1,0:T(8,128)(2,1)} fusion(bf16[16,32,4096]{2,1,0:T(8,128)(2,1)} %bitcast.50, pred[16,32]{1,0:T(8,128)(4,1)S(1)} %broadcast_in_dim.36), kind=kLoop, calls=%fused_computation.15 | loop fusion | flops 2097152 | bytes 8389120 | tf_op jit(solution)/shard_map/jit(_where)/select_n | solution.py:38
  100.2 0.0 copy-start
  100.2 0.0 all-to-all-done
  100.2 7.4 %all-to-all-start.1 = ((bf16[16,32,4096]{2,1,0:T(8,128)(2,1)}), bf16[16,32,4096]{2,1,0:T(8,128)(2,1)}, u32[]{:S(2)}, u32[]{:S(2)}) async-start(bf16[16,32,4096]{2,1,0:T(8,128)(2,1)} %broadcast_select_fusion), calls=%async_computation.1 | async-start | bytes 8388608 | tf_op jit(solution)/shard_map/all_to_all | solution.py:40
  107.6 0.0 copy-start.1
  107.6 0.0 copy-done
  107.6 2.1 all-gather
  109.8 1.3 dynamic-slice
  111.0 1.3 dynamic-slice.2
  113.6 0.1 reshape.144
  113.7 36.4 %all-to-all-done.1 = bf16[16,32,4096]{2,1,0:T(8,128)(2,1)} async-done(((bf16[16,32,4096]{2,1,0:T(8,128)(2,1)}), bf16[16,32,4096]{2,1,0:T(8,128)(2,1)}, u32[]{:S(2)}, u32[]{:S(2)}) %all-to-all-start.1) | async-done | bytes 4194336 | tf_op jit(solution)/shard_map/all_to_all | solution.py:40
  150.1 5.7 %multiply_convert_fusion = bf16[16,32,4096]{2,1,0:T(8,128)(2,1)} fusion(bf16[16,32,4096]{2,1,0:T(8,128)(2,1)} %all-to-all-done.1, f32[16,32]{1,0:T(8,128)S(1)} %bitcast.52), kind=kLoop, calls=%fused_computation.12 | loop fusion | flops 6291456 | bytes 8390656 | tf_op jit(solution)/shard_map/convert_element_type | solution.py:51
  155.9 0.0 all-gather.6.cloned.1.call-done
  155.9 0.0 copy-done.1
  155.9 8.5 %multiply_reduce_fusion = (f32[512]{0:T(512)S(1)}, bf16[512,768]{1,0:T(8,128)(2,1)}) fusion(bf16[1,1,16,32,768]{4,3,2,1,0:T(8,128)(2,1)S(1)} %copy-done.1, f32[512]{0:T(512)S(1)} %reshape.144, bf16[512,4096]{1,0:T(8,128)(2,1)} %bitcast.4, bf16[1,768,4096]{2,1,0:T(8,128)(2,1)} %all-gather.6.cloned.1.call-done, f32[4096]{0:T(1024)S(1)} %bitcast.54), kind=kOutput, calls=%fused_computation.16 | convolution fusion | flops 3235773952 | bytes 12079104 | tf_op jit(solution)/shard_map/dot_general | solution.py:60
  164.3 0.7 all_to_all.18
  165.0 10.8 %all-to-all-start.2 = ((f32[16,1,32]{2,1,0:T(1,128)}), f32[16,1,32]{2,1,0:T(1,128)S(1)}, u32[]{:S(2)}, u32[]{:S(2)}) async-start(f32[16,1,32]{2,1,0:T(1,128)} %all_to_all.18), calls=%async_computation.2 | async-start | bytes 16384 | tf_op jit(solution)/shard_map/all_to_all | solution.py:73
  175.8 9.6 %fusion.4 = f32[4096]{0:T(1024)S(1)} fusion(bf16[1,768,4096]{2,1,0:T(8,128)(2,1)} %all-gather.6.cloned.1.call-done, bf16[512,4096]{1,0:T(8,128)(2,1)} %bitcast.51, bf16[512,768]{1,0:T(8,128)(2,1)S(1)} %bitcast.59, f32[4096]{0:T(1024)S(1)} %bitcast.55), kind=kOutput, calls=%fused_computation.11 | convolution fusion | flops 3246387200 | bytes 11304960 | tf_op jit(solution)/shard_map/dot_general | solution.py:63
  185.4 3.4 %all-reduce = f32[4096]{0:T(1024)S(1)} all-reduce(f32[4096]{0:T(1024)S(1)} %fusion.4), channel_id=3, replica_groups=mesh['dp'=2,'expert'=16,'tensor'=16] {'dp'}, use_global_device_ids=true, to_apply=%region_5.6.clone | all-reduce | flops 4096 | bytes 32768
  188.7 0.0 all-to-all-done.2
  188.7 0.5 broadcast.101
  189.3 0.7 reduce.9
  189.9 0.1 reshape.142
  190.0 1.9 gather_fusion.2
  192.0 0.1 reshape.143
  192.1 53.5 %all-reduce.2 = (f32[1,2048]{1,0:T(1,128)}, f32[128,2]{1,0:T(8,128)S(1)}) all-reduce(f32[1,2048]{1,0:T(1,128)S(1)} %bitcast.53, f32[128,2]{1,0:T(8,128)S(1)} %reshape.143), channel_id=1, replica_groups=mesh['dp'=2,'expert'=16,'tensor'=16] {'tensor'}, use_global_device_ids=true, to_apply=%region_6.7 | all-reduce | flops 2304 | bytes 18432 | tf_op jit(solution)/shard_map/psum | solution.py:77
  245.6 0.6 copy.27
  (15 shorter events, 0.2 us)
Async XLA Ops:
  7.2 78.4 %all-gather.4.cloned.1.call-start = ((), (), s32[]{:S(2)}) async-start(), calls=%async_computation.3 | async-start | bytes 1114112 | tf_op jit(solution)/shard_map/all_gather | solution.py:37
  7.9 148.0 %all-gather.6.cloned.1.call-start = ((), (), s32[]{:S(2)}) async-start(), calls=%async_computation.4 | async-start | bytes 9437184 | tf_op jit(solution)/shard_map/all_gather | solution.py:53
  18.2 82.0 %all-to-all-start = ((bf16[16,1,32]{2,1,0:T(2,128)(2,1)}), bf16[16,1,32]{2,1,0:T(2,128)(2,1)S(1)}, u32[]{:S(2)}, u32[]{:S(2)}) async-start(bf16[16,1,32]{2,1,0:T(2,128)(2,1)} %all_to_all.20), calls=%async_computation | async-start | bytes 16384 | tf_op jit(solution)/shard_map/all_to_all | solution.py:47
  100.2 7.4 %copy-start = (bf16[1,2048]{1,0:T(2,128)(2,1)S(1)}, bf16[1,2048]{1,0:T(2,128)(2,1)}, u32[]{:S(2)}) copy-start(bf16[1,2048]{1,0:T(2,128)(2,1)} %param.11) | copy-start | bytes 12292
  100.2 50.0 %all-to-all-start.1 = ((bf16[16,32,4096]{2,1,0:T(8,128)(2,1)}), bf16[16,32,4096]{2,1,0:T(8,128)(2,1)}, u32[]{:S(2)}, u32[]{:S(2)}) async-start(bf16[16,32,4096]{2,1,0:T(8,128)(2,1)} %broadcast_select_fusion), calls=%async_computation.1 | async-start | bytes 8388608 | tf_op jit(solution)/shard_map/all_to_all | solution.py:40
  107.6 48.3 %copy-start.1 = (bf16[1,1,16,32,768]{4,3,2,1,0:T(8,128)(2,1)S(1)}, bf16[1,1,16,32,768]{4,3,2,1,0:T(8,128)(2,1)}, u32[]{:S(2)}) copy-start(bf16[1,1,16,32,768]{4,3,2,1,0:T(8,128)(2,1)} %param.9) | copy-start | bytes 2359300
  165.0 23.7 %all-to-all-start.2 = ((f32[16,1,32]{2,1,0:T(1,128)}), f32[16,1,32]{2,1,0:T(1,128)S(1)}, u32[]{:S(2)}, u32[]{:S(2)}) async-start(f32[16,1,32]{2,1,0:T(1,128)} %all_to_all.18), calls=%async_computation.2 | async-start | bytes 16384 | tf_op jit(solution)/shard_map/all_to_all | solution.py:73
Sparse Core Ops, SparseCore 0:
  10.1 75.4 all-gather.3
  87.6 24.1 all-gather.5
where the time goes:
time: 254 us; the launch traced here: 253 us
  waiting for transfers between devices  95.9 us (38%)
  blocking collectives  59 us (23%)
  starting transfers between devices  27.4 us (11%)
  local copies, waits for them, and re-layouts  24.7 us (10%)
  matrix products  18 us (7%)
  between operations  15.5 us (6%)
  other arithmetic  12.5 us (5%)
    all_gather x1, waiting for transfers between devices, on_device(): whole_rows = lax.all_gather(out_grad, 'tensor', axis=0, tiled=True)  58.1 us
    psum x1, blocking collectives, on_device(): scale_grad = lax.psum(own_half, 'tensor')  53.5 us
    all_to_all x1, waiting for transfers between devices, on_device(): lax.all_to_all(picked.reshape(experts, capacity, full_width), 'expert', s...  36.4 us
    all_to_all x1, starting transfers between devices, on_device(): lax.all_to_all(gate_part, 'expert', split_axis=0, concat_axis=0, tiled=True)  10.8 us
    gather x1, local copies, waits for them, and re-layouts, on_device(): whole_rows[token_slot]  10 us
    dot_general x1, matrix products, on_device(): lax.dot_general(saved_rows, scaled, (((0,), (0,)), ((), ())), preferred_e...  9.57 us
    all_to_all x1, starting transfers between devices, on_device(): lax.all_to_all(gate_slot, 'expert', split_axis=0, concat_axis=0, tiled=True)  9.19 us
    dot_general x1, matrix products, on_device(): lax.dot_general(slot_rows, quantized, (((1,), (1,)), ((), ())), preferred...  8.46 us
  transfers between devices with their start and end apart: 5, of which 2 were waited for; matrix products, arithmetic and copies ran while one was open for 16% of the time, Pallas kernels for 0%

commit v1 on v0

v1 whole, which is shorter than its diff:
```python
import functools
import math

import jax
import jax.numpy as jnp
from jax import lax
from jax.experimental import pallas as pl
from jax.experimental.pallas import tpu as pltpu
from jax.sharding import PartitionSpec as P

MESH = pl.DeviceIdType.MESH
F32 = jnp.float32
BF16 = jnp.bfloat16
LANES = 128


def remote(src, dst, send_sem, recv_sem, device):
    return pltpu.make_async_remote_copy(
        src_ref=src,
        dst_ref=dst,
        send_sem=send_sem,
        recv_sem=recv_sem,
        device_id=device,
        device_id_type=MESH,
    )


def iota(shape, axis):
    return lax.broadcasted_iota(jnp.int32, shape, axis)


def kernel(
    nt, ne, cap, units, half,
    og, rt, gc, cs, hs, dw,
    hg_out, sg_out, gg_out,
    W, S, HS, QZ, SL, TM, TOKP, SRCP, QT, PMSG, PX, XP, QS, XQ, ACC, GB,
    SPART, SRECV, SX, SY, SALL, GM, GV, PV, PVR,
    lsem, wsem, ssem, zsem, qrsem, qlsem, pxsem, prsem, plsem, xqsem,
    gxsem, gzsem, srsem, sxsem, sasem,
):
    d = lax.axis_index("dp")
    e = lax.axis_index("expert")
    t = lax.axis_index("tensor")
    side = math.isqrt(ne)
    ex, ey = lax.div(e, side), lax.rem(e, side)
    group = 8 * nt
    slots = ne * cap
    phalf = (nt // 2) * LANES
    qhalf = half - phalf
    n_right, n_left = nt // 2, nt // 2 - 1
    other = 1 - d

    def zpeer(k):
        return lax.rem(t + k + nt, nt)

    def xpeer(o):
        return lax.rem(ex + o // side, side) * side + lax.rem(ey + o % side, side)

    partner = (other, e, t)

    load_w = pltpu.make_async_copy(dw, W.at[d], lsem.at[0])
    load_h = pltpu.make_async_copy(hs, HS, lsem.at[1])
    load_w.start()
    load_h.start()

    barrier = pltpu.get_barrier_semaphore()
    pl.semaphore_signal(barrier, inc=1, device_id=partner, device_id_type=MESH)
    for k in range(1, nt):
        pl.semaphore_signal(barrier, inc=1, device_id=(d, e, zpeer(k)), device_id_type=MESH)
    for o in range(1, ne):
        pl.semaphore_signal(barrier, inc=1, device_id=(d, xpeer(o), t), device_id_type=MESH)

    S[d] = jnp.broadcast_to(cs[...].astype(F32), (8, half))
    for j in range(nt):
        start = (j // (nt // 2)) * half + (j % (nt // 2)) * LANES
        SRCP[j] = og[:, start : start + LANES].astype(F32)
    TOKP[t] = SRCP[t]
    QT[t] = jnp.concatenate(
        [og[:, phalf:half].astype(F32), og[:, half + phalf : 2 * half].astype(F32)], axis=0
    ).astype(BF16)

    pl.semaphore_wait(barrier, nt + ne - 1)

    started = []

    def go(copy):
        copy.start()
        started.append(copy)
        return copy

    right, left = (d, e, zpeer(1)), (d, e, zpeer(-1))
    go(remote(QT.at[t], QT.at[t], qrsem.at[0, 1], qrsem.at[1, 1], right))
    go(remote(QT.at[t], QT.at[t], qlsem.at[0, 1], qlsem.at[1, 1], left))
    for k in range(1, nt):
        go(remote(SRCP.at[zpeer(k)], TOKP.at[t], zsem.at[0, k], zsem.at[1, k], (d, e, zpeer(k))))
    go(remote(S.at[d], S.at[d], ssem.at[0], ssem.at[1], partner))
    go(remote(dw, W.at[d], wsem.at[0], wsem.at[1], partner))

    def ring_q(k):
        jr, jl = zpeer(-k), zpeer(k)
        remote(QT.at[jr], QT.at[jr], qrsem.at[0, k], qrsem.at[1, k], right).wait_recv()
        if k < n_right:
            go(remote(QT.at[jr], QT.at[jr], qrsem.at[0, k + 1], qrsem.at[1, k + 1], right))
        if k <= n_left:
            remote(QT.at[jl], QT.at[jl], qlsem.at[0, k], qlsem.at[1, k], left).wait_recv()
            if k < n_left:
                go(remote(QT.at[jl], QT.at[jl], qlsem.at[0, k + 1], qlsem.at[1, k + 1], left))

    wide = 2 * group + group
    column = iota((group, wide), 1)
    token_of = jnp.where(
        column < 2 * group,
        lax.shift_right_logical(column, 4) * 8 + jnp.bitwise_and(column, 7),
        column - 2 * group,
    )
    row = iota((group, wide), 0)
    same = row == token_of
    earlier = jnp.where(row < token_of, 1.0, 0.0).astype(BF16)
    routes = rt[...].astype(F32)
    codes = gc[...].astype(F32)
    name = [jnp.sum(jnp.where(same, routes[:, k : k + 1], 0.0), axis=0, keepdims=True) for k in (0, 1)]
    gate = [
        jnp.sum(jnp.where(same, codes[:, k : k + 1], 0.0), axis=0, keepdims=True)[:, 2 * group :]
        for k in (0, 1)
    ]
    expert_row = iota((ne, wide), 0).astype(F32)
    names = [jnp.where(expert_row == name[k], 1.0, 0.0) for k in (0, 1)]
    both = (names[0] + names[1])[:, 2 * group :].astype(BF16)
    before = jnp.dot(both, earlier, preferred_element_type=F32)
    place = [jnp.sum(names[k] * before, axis=0, keepdims=True) for k in (0, 1)]
    slot = [name[k] * float(cap) + place[k] for k in (0, 1)]
    slot_row = iota((slots, wide), 0).astype(F32)
    picks = [jnp.where(slot_row == slot[k], 1.0, 0.0) for k in (0, 1)]
    pick = picks[0] + picks[1]
    pick_p = pick[:, 2 * group :].astype(BF16)
    in_half = jnp.bitwise_and(lax.shift_right_logical(iota((slots, 2 * group), 1), 3), 1)
    pick_q = [jnp.where(in_half == a, pick[:, : 2 * group], 0.0).astype(BF16) for a in (0, 1)]
    gate_pick = (
        picks[0][:, 2 * group :] * gate[0] + picks[1][:, 2 * group :] * gate[1]
    ).astype(BF16)
    gates = jnp.dot(gate_pick, jnp.ones((group, LANES), BF16), preferred_element_type=F32)
    gates = (gates * (1.0 / 256.0)).astype(BF16)

    ring_q(1)

    for k in range(1, nt):
        remote(SRCP.at[t], TOKP.at[zpeer(-k)], zsem.at[0, k], zsem.at[1, k], right).wait_recv()
    tokens = TOKP[...].reshape(group, LANES).astype(BF16)
    routed = jnp.dot(pick_p, tokens, preferred_element_type=F32).astype(BF16)
    PMSG[:, :cap, :] = routed.reshape(ne, cap, LANES)
    PMSG[:, cap:, :] = gates.reshape(ne, cap, LANES)
    PX[e] = PMSG[e]
    for o in range(1, ne):
        go(remote(PMSG.at[xpeer(o)], PX.at[e], pxsem.at[0, o], pxsem.at[1, o], (d, xpeer(o), t)))

    load_w.wait()
    load_h.wait()

    def unit(hh, block):
        lanes = slice(block * 256, block * 256 + 256)
        scale = S[hh, 0:1, lanes]
        inverse = 1.0 / scale

        def rows(i, carry):
            at = pl.ds(pl.multiple_of(i * 128, 128), 128)
            u = W[hh, at, lanes].astype(F32) * inverse
            b = jnp.tanh(u)
            QZ[hh, at, lanes] = (scale * b).astype(BF16)
            SL[at, :] = (b - u * (1.0 - b * b)).astype(BF16)
            return carry

        lax.fori_loop(0, units // 128, rows, 0)
        TM[hh, :, lanes] = jnp.dot(HS[...], SL[...], preferred_element_type=F32)

    n_units = half // 256
    work = [(d, b) for b in range(n_units)]
    work_other = [(other, b) for b in range(n_units)]

    def do(n):
        for _ in range(n):
            if work:
                unit(*work.pop(0))

    ring_q(2)
    do(1)
    for k in range(3, n_right):
        ring_q(k)
        if k == n_right - 3:
            pass
        do(1)
    for o in range(1, ne):
        remote(PMSG.at[e], PX.at[xpeer(ne - o)], pxsem.at[0, o], pxsem.at[1, o], right).wait_recv()
    XP[t] = PX[:, :cap, :].reshape(slots, LANES)
    GB[...] = PX[:, cap:, :].reshape(slots, LANES).astype(F32)
    pieces = 2
    prow = slots // pieces

    def piece(j, i):
        return XP.at[j, pl.ds(i * prow, prow)]

    for i in range(pieces):
        go(remote(piece(t, i), piece(t, i), prsem.at[0, 1, i], prsem.at[1, 1, i], right))
        go(remote(piece(t, i), piece(t, i), plsem.at[0, 1, i], plsem.at[1, 1, i], left))

    def ring_p(k):
        jr, jl = zpeer(-k), zpeer(k)
        for i in range(pieces):
            remote(piece(jr, i), piece(jr, i), prsem.at[0, k, i], prsem.at[1, k, i], right).wait_recv()
            if k < n_right:
                go(remote(piece(jr, i), piece(jr, i), prsem.at[0, k + 1, i], prsem.at[1, k + 1, i], right))
            if k <= n_left:
                remote(piece(jl, i), piece(jl, i), plsem.at[0, k, i], plsem.at[1, k, i], left).wait_recv()
                if k < n_left:
                    go(remote(piece(jl, i), piece(jl, i), plsem.at[0, k + 1, i], plsem.at[1, k + 1, i], left))

    if n_right > 2:
        ring_q(n_right)

    for a in (0, 1):
        gathered = QT[...].reshape(2 * group, qhalf)
        step = 256
        for c in range(0, qhalf, step):
            QS[a, :, :, c : c + step] = (
                jnp.dot(pick_q[a], gathered[:, c : c + step], preferred_element_type=F32)
                .astype(BF16)
                .reshape(ne, cap, step)
            )
        for o in range(1, ne):
            go(remote(QS.at[a, xpeer(o)], XQ.at[a, e], xqsem.at[0, a, o], xqsem.at[1, a, o], (d, xpeer(o), t)))
        XQ[a, e] = QS[a, e]

    ACC[...] = jnp.zeros_like(ACC)

    def terms(x, hh, start):
        scaled = (x.astype(F32) * GB[...]).astype(BF16).astype(F32)
        return jnp.sum(scaled * TM[hh, :, pl.ds(start, LANES)], axis=0, keepdims=True)

    def chunk_p(js):
        xs, qs = [], []
        for j in js:
            hh = lax.div(j, nt // 2)
            b = lax.rem(j, nt // 2)
            start = pl.multiple_of(b * LANES, LANES)
            x = XP[j]
            SPART[b, pl.ds(hh, 1), :] = terms(x, hh, start)
            xs.append(x)
            qs.append(QZ[hh, :, pl.ds(start, LANES)])
        x = xs[0] if len(xs) == 1 else jnp.concatenate(xs, axis=1)
        q = qs[0] if len(qs) == 1 else jnp.concatenate(qs, axis=1)
        ACC[...] += lax.dot_general(x, q, (((1,), (1,)), ((), ())), preferred_element_type=F32)

    ring_p(1)
    do(n_units)
    remote(S.at[d], S.at[other], ssem.at[0], ssem.at[1], partner).wait_recv()
    remote(dw, W.at[other], wsem.at[0], wsem.at[1], partner).wait_recv()
    work.extend(work_other)
    per = -(-n_units // 4)
    for k in range(2, 6):
        if k <= n_right:
            ring_p(k)
        do(per)
    do(n_units)
    chunk_p([t])
    for k in range(1, min(5, n_right)):
        chunk_p([zpeer(-k), zpeer(k)])
    for k in range(6, n_right + 1):
        ring_p(k)
        chunk_p([zpeer(1 - k), zpeer(k - 1)])
    if n_right >= 2 and n_right < 6:
        chunk_p([zpeer(1 - n_right), zpeer(n_right - 1)]) if n_right == 5 else None
    chunk_p([zpeer(n_right)])

    def send_terms(k):
        go(remote(SPART.at[zpeer(k)], SRECV.at[t], srsem.at[0, k], srsem.at[1, k], (d, e, zpeer(k))))

    for a in (0, 1):
        for o in range(1, ne):
            remote(QS.at[a, e], XQ.at[a, xpeer(ne - o)], xqsem.at[0, a, o], xqsem.at[1, a, o], right).wait_recv()
        for c in range(0, qhalf, LANES):
            x = XQ[a, :, :, c : c + LANES].reshape(slots, LANES)
            SPART[nt // 2 + c // LANES, a : a + 1, :] = terms(x, a, phalf + c)
        if a == 1:
            SRECV[t] = SPART[t]
            for k in range(1, nt):
                send_terms(k)
        ACC[...] += lax.dot_general(
            XQ[a].reshape(slots, qhalf),
            QZ[a, :, phalf:half],
            (((1,), (1,)), ((), ())),
            preferred_element_type=F32,
        )

    weighed = ACC[:, 0:LANES] * HS[:, 0:LANES].astype(F32)
    for c in range(LANES, units, LANES):
        weighed += ACC[:, c : c + LANES] * HS[:, c : c + LANES].astype(F32)
    weighed = jnp.sum(weighed, axis=1, keepdims=True)
    at_place = jnp.bitwise_and(iota((slots, LANES), 0), cap - 1) == iota((slots, LANES), 1)
    GM[...] = jnp.sum(
        jnp.where(at_place, weighed, 0.0).reshape(ne, cap, LANES), axis=1, keepdims=True
    )
    GV[e] = GM[e]
    for o in range(1, ne):
        go(remote(GM.at[xpeer(o)], GV.at[e], gxsem.at[0, o], gxsem.at[1, o], (d, xpeer(o), t)))

    for k in range(1, nt):
        remote(SPART.at[t], SRECV.at[zpeer(-k)], srsem.at[0, k], srsem.at[1, k], right).wait_recv()
    total = SRECV[0]
    for i in range(1, nt):
        total += SRECV[i]
    SX[0] = total[0:1]
    SX[1] = total[1:2]
    go(remote(SX.at[other], SY, sxsem.at[0], sxsem.at[1], partner))

    for c in range(0, units, LANES):
        hg_out[:, c : c + LANES] = (ACC[:, c : c + LANES] * GB[...]).astype(BF16)

    remote(SX.at[d], SY, sxsem.at[0], sxsem.at[1], partner).wait_recv()
    SALL[t] = SX[d] + SY[...]
    for k in range(1, nt):
        go(remote(SALL.at[t], SALL.at[t], sasem.at[0, k], sasem.at[1, k], (d, e, zpeer(k))))

    for o in range(1, ne):
        remote(GM.at[e], GV.at[xpeer(ne - o)], gxsem.at[0, o], gxsem.at[1, o], right).wait_recv()
    values = jnp.concatenate([GV[i] for i in range(ne)], axis=0)
    place_row = iota((LANES, group), 0).astype(F32)
    pair_rows = []
    for k in (0, 1):
        chosen = jnp.where(place_row == place[k][:, 2 * group :], 1.0, 0.0)
        spread = jnp.dot(values, chosen, precision=lax.Precision.HIGHEST, preferred_element_type=F32)
        pair_rows.append(jnp.sum(spread * names[k][:, 2 * group :], axis=0, keepdims=True))
    PV[...] = jnp.concatenate(pair_rows, axis=0)
    PVR[t] = PV[...]
    for k in range(1, nt):
        go(remote(PV, PVR.at[t], gzsem.at[0, k], gzsem.at[1, k], (d, e, zpeer(k))))

    for k in range(1, nt):
        remote(SALL.at[t], SALL.at[zpeer(-k)], sasem.at[0, k], sasem.at[1, k], right).wait_recv()
    for i in range(nt):
        sg_out[:, i * LANES : (i + 1) * LANES] = SALL[i]

    for k in range(1, nt):
        remote(PV, PVR.at[zpeer(-k)], gzsem.at[0, k], gzsem.at[1, k], right).wait_recv()
    total = PVR[0]
    for i in range(1, nt):
        total += PVR[i]
    mine = iota((8, group), 1) == t * 8 + iota((8, group), 0)
    pair = [jnp.sum(jnp.where(mine, total[k : k + 1], 0.0), axis=1, keepdims=True) for k in (0, 1)]
    gg_out[...] = jnp.concatenate(pair, axis=1)

    for copy in started:
        copy.wait_send()


def on_device(nt, ne, out_grad, routing, gate_codes, hidden_saved, down_weight, channel_scale):
    cap = hidden_saved.shape[3]
    units = hidden_saved.shape[4]
    half = down_weight.shape[2]
    group = routing.shape[0]
    slots = ne * cap
    phalf = (nt // 2) * LANES
    qhalf = half - phalf
    vmem = pl.BlockSpec(memory_space=pltpu.VMEM)
    anywhere = pl.BlockSpec(memory_space=pl.ANY)
    dma = pltpu.SemaphoreType.DMA
    hidden_grad, scale_grad, gate_grad = pl.pallas_call(
        functools.partial(kernel, nt, ne, cap, units, half),
        out_shape=(
            jax.ShapeDtypeStruct((slots, units), BF16),
            jax.ShapeDtypeStruct((1, half), F32),
            jax.ShapeDtypeStruct((8, 2), F32),
        ),
        in_specs=[vmem, vmem, vmem, vmem, anywhere, anywhere],
        out_specs=(vmem, vmem, vmem),
        scratch_shapes=[
            pltpu.VMEM((2, units, half), BF16),
            pltpu.VMEM((2, 8, half), F32),
            pltpu.VMEM((slots, units), BF16),
            pltpu.VMEM((2, units, half), BF16),
            pltpu.VMEM((units, 256), BF16),
            pltpu.VMEM((2, slots, half), F32),
            pltpu.VMEM((nt, 8, LANES), F32),
            pltpu.VMEM((nt, 8, LANES), F32),
            pltpu.VMEM((nt, 16, qhalf), BF16),
            pltpu.VMEM((ne, 2 * cap, LANES), BF16),
            pltpu.VMEM((ne, 2 * cap, LANES), BF16),
            pltpu.VMEM((nt, slots, LANES), BF16),
            pltpu.VMEM((2, ne, cap, qhalf), BF16),
            pltpu.VMEM((2, ne, cap, qhalf), BF16),
            pltpu.VMEM((slots, units), F32),
            pltpu.VMEM((slots, LANES), F32),
            pltpu.VMEM((nt, 2, LANES), F32),
            pltpu.VMEM((nt, 2, LANES), F32),
            pltpu.VMEM((2, 1, LANES), F32),
            pltpu.VMEM((1, LANES), F32),
            pltpu.VMEM((nt, 1, LANES), F32),
            pltpu.VMEM((ne, 1, LANES), F32),
            pltpu.VMEM((ne, 1, LANES), F32),
            pltpu.VMEM((2, LANES if group == LANES else group), F32),
            pltpu.VMEM((nt, 2, group), F32),
            dma((2,)),
            dma((2,)),
            dma((2,)),
            dma((2, nt)),
            dma((2, nt // 2 + 1)),
            dma((2, nt // 2 + 1)),
            dma((2, ne)),
            dma((2, nt // 2 + 1, 2)),
            dma((2, nt // 2 + 1, 2)),
            dma((2, 2, ne)),
            dma((2, ne)),
            dma((2, nt)),
            dma((2, nt)),
            dma((2,)),
            dma((2, nt)),
        ],
        compiler_params=pltpu.CompilerParams(
            collective_id=0, has_side_effects=True, vmem_limit_bytes=60 * 1024 * 1024
        ),
    )(
        out_grad,
        routing,
        gate_codes,
        channel_scale,
        hidden_saved.reshape(slots, units),
        down_weight.reshape(units, half),
    )
    return hidden_grad.reshape(hidden_saved.shape), scale_grad, gate_grad


def solution(mesh):
    in_specs = (
        P(("dp", "expert", "tensor"), None),
        P(("dp", "expert"), None),
        P(("dp", "expert"), None),
        P("dp", "expert", None, None, "tensor"),
        P("expert", "tensor", "dp"),
        P("expert", "dp"),
    )
    out_specs = (
        P("dp", "expert", None, None, "tensor"),
        P("expert", "dp"),
        P(("dp", "expert", "tensor"), None),
    )
    return jax.shard_map(
        functools.partial(on_device, mesh.shape["tensor"], mesh.shape["expert"]),
        mesh=mesh,
        in_specs=in_specs,
        out_specs=out_specs,
        check_vma=False,
    )
```

time: 254 us -> 105 us (0.41)
  waiting for transfers between devices: 95.9 us -> 0 us
  Pallas kernels: 0 us -> 95.3 us
  blocking collectives: 59 us -> 0 us
  starting transfers between devices: 27.4 us -> 0 us
  matrix products: 18 us -> 0 us
  local copies, waits for them, and re-layouts: 24.7 us -> 7.5 us
  between operations: 15.5 us -> 0.64 us
  other arithmetic: 12.5 us -> 0 us
    pallas_call x0 -> x1, Pallas kernels: none -> 95.3 us  [on_device(): pl.pallas_call(functools.partial(kernel, nt, ne, cap, units, half), out_s...]
    all_gather x2 -> x0, waiting for transfers between devices: 58.1 us -> none  [the longest x1 58.1 us: on_device(): whole_rows = lax.all_gather(out_grad, 'tensor', axis=0, tiled=True)]
    psum x1 -> x0, blocking collectives: 53.5 us -> none  [on_device(): scale_grad = lax.psum(own_half, 'tensor')]
    all_to_all x3 -> x0, waiting for transfers between devices: 36.4 us -> none  [the longest x1 36.4 us: on_device(): lax.all_to_all(picked.reshape(experts, capacity, full_width), 'expert', s...]
    all_to_all x3 -> x0, starting transfers between devices: 27.4 us -> none  [the longest x1 10.8 us: on_device(): lax.all_to_all(gate_part, 'expert', split_axis=0, concat_axis=0, tiled=True)]
    dot_general x2 -> x0, matrix products: 18 us -> none  [the longest x1 9.57 us: on_device(): lax.dot_general(saved_rows, scaled, (((0,), (0,)), ((), ())), preferred_e...]
    gather x3 -> x0, local copies, waits for them, and re-layouts: 15.5 us -> none  [the longest x1 10 us: on_device(): whole_rows[token_slot]]
    convert_element_type x6 -> x0, other arithmetic: 5.78 us -> none  [the longest x1 5.72 us: on_device(): scaled = (gate_rows[:, None] * slot_rows).astype(jnp.bfloat16)]
  transfers between devices with their start and end apart: 5 -> 0, of which waited for: 2 -> 0; matrix products, arithmetic and copies ran while one was open for 16% -> 0% of each run, Pallas kernels for 0% -> 0%
where the time goes in v1:
time: 105 us; the launch traced here: 103 us
  Pallas kernels  95.3 us (91%)
  local copies, waits for them, and re-layouts  7.5 us (7%)
    pallas_call x1, Pallas kernels, on_device(): pl.pallas_call(functools.partial(kernel, nt, ne, cap, units, half), out_s...  95.3 us
    unnamed x5, local copies, waits for them, and re-layouts  7.5 us

profile of v1, /device:TPU:6, one launch (start us, length us, event | category | flops | bytes accessed | tf_op | source)
XLA Modules:
  0.0 103.5 jit_solution(14594929648285443807)
XLA Ops:
  0.6 1.4 %copy.9.rt = s32[128,2]{1,0:T(8,128)} copy(s32[128,2]{0,1:T(2,128)} %param.7) | data formatting | bytes 2048 | tf_op args[1]
  2.0 1.4 %copy.10.gc = s32[128,2]{1,0:T(8,128)} copy(s32[128,2]{0,1:T(2,128)} %param.8) | data formatting | bytes 2048 | tf_op args[2]
  3.5 95.3 %shard_map.85 = (bf16[512,768]{1,0:T(8,128)(2,1)}, f32[1,2048]{1,0:T(1,128)}, f32[8,2]{1,0:T(8,128)}) custom-call(bf16[8,4096]{1,0:T(8,128)(2,1)} %og.1, s32[128,2]{1,0:T(8,128)} %copy.9.rt, s32[128,2]{1,0:T(8,128)} %copy.10.gc, bf16[1,2048]{1,0:T(2,128)(2,1)} %cs.1, bf16[512,768]{1,0:T(8,128)(2,1)} %bitcast.5, bf16[768,2048]{1,0:T(8,128)(2,1)} %bitcast.3), custom_call_target="tpu_custom_call" | custom-call | tf_op jit(solution)/shard_map/pallas_call | solution.py:365
  98.8 1.3 %copy.11 = f32[8,2]{0,1:T(2,128)} copy(f32[8,2]{1,0:T(8,128)} %get-tuple-element.11) | data formatting | bytes 128
  100.1 2.1 %copy.14 = bf16[1,1,16,32,768]{4,3,2,1,0:T(8,128)(2,1)} copy(bf16[1,1,16,32,768]{4,3,2,1,0:T(8,128)(2,1)} %bitcast.4) | data formatting | bytes 1572864
  102.2 1.3 %copy.15 = f32[1,2048]{1,0:T(1,128)} copy(f32[1,2048]{1,0:T(1,128)} %get-tuple-element.16) | data formatting | bytes 16384

commit v2 on v1

v2 whole, which is shorter than its diff:
```python
import functools
import math

import jax
import jax.numpy as jnp
from jax import lax
from jax.experimental import pallas as pl
from jax.experimental.pallas import tpu as pltpu
from jax.sharding import PartitionSpec as P

MESH = pl.DeviceIdType.MESH
F32 = jnp.float32
BF16 = jnp.bfloat16
LANES = 128


def remote(src, dst, send_sem, recv_sem, device):
    return pltpu.make_async_remote_copy(
        src_ref=src,
        dst_ref=dst,
        send_sem=send_sem,
        recv_sem=recv_sem,
        device_id=device,
        device_id_type=MESH,
    )


def iota(shape, axis):
    return lax.broadcasted_iota(jnp.int32, shape, axis)


def gather_plan(nt):
    if nt == 16:
        return {0: (8, 4, -4, 1, -1, 2, -2), -4: (1, -1, 2), 4: (1, -1, -2), 8: (1, -1)}
    return {0: tuple(range(1, nt))}


def kernel(
    nt, ne, cap, units, half,
    og, rt, gc, cs, hs, dw,
    hg_out, sg_out, gg_out,
    W, S, HS, QZ, SL, TM, TOKP, SRCP, QT, PMSG, PX, XP, QS, XQ, ACC, GB, HG,
    SPART, SPX, SSUM, SRECV, GM, GV, PV, PVR,
    lsem, wsem, ssem, zsem, qasem, qbsem, pxsem, prsem, psend, xqsem,
    gxsem, gzsem, spsem, srsem,
):
    d = lax.axis_index("dp")
    e = lax.axis_index("expert")
    t = lax.axis_index("tensor")
    side = math.isqrt(ne)
    ex, ey = lax.div(e, side), lax.rem(e, side)
    group = 8 * nt
    slots = ne * cap
    n_chunks = nt // 2
    chunk_w = 2 * LANES
    per_half = n_chunks // 2
    phalf = per_half * chunk_w
    qhalf = half - phalf
    part = qhalf // 2
    blocks = half // LANES
    reach = n_chunks // 2
    other = 1 - d

    def zpeer(k):
        return lax.rem(t + k + nt, nt)

    def xpeer(o):
        return lax.rem(ex + o // side, side) * side + lax.rem(ey + o % side, side)

    def at_z(k):
        return (d, e, zpeer(k))

    def at_x(o):
        return (d, xpeer(o), t)

    partner = (other, e, t)
    right, left = at_z(1), at_z(-1)

    def arrived(ref, sems):
        remote(ref, ref, sems.at[0], sems.at[1], partner).wait_recv()

    def left_here(ref, sems):
        remote(ref, ref, sems.at[0], sems.at[1], partner).wait_send()

    load_w = pltpu.make_async_copy(dw, W.at[d], lsem.at[0])
    load_h = pltpu.make_async_copy(hs, HS, lsem.at[1])
    load_w.start()
    load_h.start()

    barrier = pltpu.get_barrier_semaphore()
    for k in range(1, nt):
        pl.semaphore_signal(barrier, inc=1, device_id=at_z(k), device_id_type=MESH)
    for o in range(1, ne):
        pl.semaphore_signal(barrier, inc=1, device_id=at_x(o), device_id_type=MESH)
    pl.semaphore_signal(barrier, inc=1, device_id=partner, device_id_type=MESH)

    def two_rows(first, second, width):
        upper = og[:, first : first + width].astype(F32)
        lower = og[:, second : second + width].astype(F32)
        return jnp.concatenate([upper, lower], axis=0).astype(BF16)

    for i in (0, 1):
        QT[i, t] = two_rows(phalf + i * part, half + phalf + i * part, part)
    for j in range(n_chunks):
        start = (j // per_half) * half + (j % per_half) * chunk_w
        SRCP[j] = two_rows(start, start + LANES, LANES)
    TOKP[t] = SRCP[lax.rem(t, n_chunks)]
    S[d] = jnp.broadcast_to(cs[...].astype(F32), (8, half))

    pl.semaphore_wait(barrier, nt + ne - 1)

    plan = gather_plan(nt)
    via = [rel for rel in plan if rel]

    def send_tokens(i, rel, offsets):
        chunk = QT.at[i, zpeer(rel)]
        for k in offsets:
            seen = -k if k != 8 else 8
            recv = qasem.at[i, via.index(seen)] if rel == 0 and seen in via else qbsem.at[i, 1]
            remote(chunk, chunk, qbsem.at[i, 0], recv, at_z(k)).start()

    def tokens_from(i, rel):
        chunk = QT.at[i, zpeer(rel)]
        remote(chunk, chunk, qbsem.at[i, 0], qasem.at[i, via.index(rel)], partner).wait_recv()
        send_tokens(i, rel, plan[rel])

    send_tokens(0, 0, plan[0][:3])
    for k in range(1, nt):
        source = SRCP.at[lax.rem(zpeer(k), n_chunks)]
        remote(source, TOKP.at[t], zsem.at[0], zsem.at[1], at_z(k)).start()
    send_tokens(0, 0, plan[0][3:])
    send_tokens(1, 0, plan[0])
    remote(S.at[d], S.at[d], ssem.at[0], ssem.at[1], partner).start()
    remote(dw, W.at[d], wsem.at[0], wsem.at[1], partner).start()

    wide = 2 * group + group
    column = iota((group, wide), 1)
    token_of = jnp.where(
        column < 2 * group,
        lax.shift_right_logical(column, 4) * 8 + jnp.bitwise_and(column, 7),
        column - 2 * group,
    )
    row = iota((group, wide), 0)
    same = jnp.where(row == token_of, 1.0, 0.0).astype(BF16)
    earlier = jnp.where(row < token_of, 1.0, 0.0).astype(BF16)
    routes = jnp.dot(rt[...].astype(F32).astype(BF16), same, preferred_element_type=F32)
    codes = gc[...].astype(F32)
    name = [routes[k : k + 1] for k in (0, 1)]
    gate = [codes[k : k + 1] for k in (0, 1)]
    expert_row = iota((ne, wide), 0).astype(F32)
    names = [jnp.where(expert_row == name[k], 1.0, 0.0) for k in (0, 1)]
    both = (names[0] + names[1])[:, 2 * group :].astype(BF16)
    before = jnp.dot(both, earlier, preferred_element_type=F32)
    place = [jnp.sum(names[k] * before, axis=0, keepdims=True) for k in (0, 1)]
    slot = [name[k] * float(cap) + place[k] for k in (0, 1)]
    slot_row = iota((slots, wide), 0).astype(F32)
    picks = [jnp.where(slot_row == slot[k], 1.0, 0.0) for k in (0, 1)]
    pick = picks[0] + picks[1]
    in_half = jnp.bitwise_and(lax.shift_right_logical(iota((slots, 2 * group), 1), 3), 1)
    pick_q = [jnp.where(in_half == a, pick[:, : 2 * group], 0.0).astype(BF16) for a in (0, 1)]
    gate_pick = (
        picks[0][:, 2 * group :] * gate[0] + picks[1][:, 2 * group :] * gate[1]
    ).astype(BF16)
    gates = jnp.dot(gate_pick, jnp.ones((group, LANES), BF16), preferred_element_type=F32)
    PMSG[:, 2 * cap :, :] = (gates * (1.0 / 256.0)).astype(BF16).reshape(ne, cap, LANES)

    load_w.wait()
    load_h.wait()

    def unit(hh, block):
        lanes = slice(block * 256, block * 256 + 256)
        scale = S[hh, 0:1, lanes]
        inverse = 1.0 / scale

        def rows(i, carry):
            at = pl.ds(pl.multiple_of(i * 128, 128), 128)
            u = W[hh, at, lanes].astype(F32) * inverse
            b = jnp.tanh(u)
            QZ[hh, at, lanes] = (scale * b).astype(BF16)
            SL[at, :] = (b - u * (1.0 - b * b)).astype(BF16)
            return carry

        lax.fori_loop(0, units // 128, rows, 0)
        TM[hh, :, lanes] = jnp.dot(HS[...], SL[...], preferred_element_type=F32)

    def partner_ready():
        arrived(S.at[other], ssem)
        arrived(W.at[other], wsem)

    def terms(x, hh, start):
        scaled = (x.astype(F32) * GB[...]).astype(BF16).astype(F32)
        return jnp.sum(scaled * TM[hh, :, pl.ds(start, LANES)], axis=0, keepdims=True)

    def chunk_p(j):
        hh = lax.div(j, per_half)
        b = lax.rem(j, per_half)
        start = pl.multiple_of(b * chunk_w, chunk_w)
        for i in (0, 1):
            x = XP[j, :, i * LANES : (i + 1) * LANES]
            SPART[hh, 2 * b + i] = terms(x, hh, pl.multiple_of(start + i * LANES, LANES))
        ACC[...] += lax.dot_general(
            XP[j],
            QZ[hh, :, pl.ds(start, chunk_w)],
            (((1,), (1,)), ((), ())),
            preferred_element_type=F32,
        )

    def parts_q(i):
        arrived(XQ.at[i, pl.ds(0, ne - 1)], xqsem.at[i])
        for a in (0, 1):
            for c in range(part // LANES):
                at = i * part + c * LANES
                x = XQ[i, :, :, a * part + c * LANES : a * part + (c + 1) * LANES]
                SPART[a, (phalf + at) // LANES] = terms(x.reshape(slots, LANES), a, phalf + at)

    def dot_q(i):
        for a in (0, 1):
            ACC[...] += lax.dot_general(
                XQ[i, :, :, a * part : (a + 1) * part].reshape(slots, part),
                QZ[a, :, phalf + i * part : phalf + (i + 1) * part],
                (((1,), (1,)), ((), ())),
                preferred_element_type=F32,
            )

    pb, qb = phalf // 256, qhalf // 256
    work = [functools.partial(unit, d, b) for b in range(pb)]
    work += [partner_ready]
    work += [functools.partial(unit, other, b) for b in range(pb)]
    work += [functools.partial(unit, h, pb + b) for b in range(qb) for h in (d, other)]
    chunks = [functools.partial(chunk_p, lax.rem(t, n_chunks))]
    for k in range(1, reach):
        for rel in (-k, k):
            chunks += [functools.partial(chunk_p, lax.rem(zpeer(rel), n_chunks))]
    chunks += [functools.partial(chunk_p, lax.rem(zpeer(reach), n_chunks))]

    def do(jobs, n):
        for _ in range(n):
            if jobs:
                jobs.pop(0)()


    do(work, 2)
    for rel in via[:2]:
        tokens_from(0, rel)

    arrived(TOKP.at[pl.ds(0, nt - 1)], zsem)
    tokens = TOKP[...].reshape(2 * group, LANES)
    for a in (0, 1):
        routed = jnp.dot(pick_q[a], tokens, preferred_element_type=F32).astype(BF16)
        PMSG[:, a * cap : (a + 1) * cap, :] = routed.reshape(ne, cap, LANES)
    for o in range(1, ne):
        remote(PMSG.at[xpeer(o)], PX.at[e], pxsem.at[0], pxsem.at[1], at_x(o)).start()
    PX[e] = PMSG[e]

    for rel in via[2:]:
        tokens_from(0, rel)
    for rel in via:
        tokens_from(1, rel)
    do(work, 2)

    n_direct = nt - 1 - len(via)

    def route_q(i):
        arrived(QT.at[i, pl.ds(0, n_direct)], qbsem.at[i])
        gathered = QT[i].reshape(2 * group, part)
        step = min(256, part)
        for a in (0, 1):
            for c in range(0, part, step):
                QS[i, :, :, a * part + c : a * part + c + step] = (
                    jnp.dot(pick_q[a], gathered[:, c : c + step], preferred_element_type=F32)
                    .astype(BF16)
                    .reshape(ne, cap, step)
                )
        for o in range(1, ne):
            remote(QS.at[i, xpeer(o)], XQ.at[i, e], xqsem.at[i, 0], xqsem.at[i, 1], at_x(o)).start()
        XQ[i, e] = QS[i, e]

    route_q(0)

    pieces = 4
    prow = slots // pieces

    def piece(j, i):
        return XP.at[j, pl.ds(i * prow, prow)]

    def pass_on(way, rel, k, i):
        if k == reach and (i < pieces // 2) != (way == 0):
            return
        ref = piece(lax.rem(zpeer(rel), n_chunks), i)
        remote(ref, ref, psend.at[way], prsem.at[way, k, i], (right, left)[way]).start()

    def ring_p(k):
        for i in range(pieces):
            for way in (0, 1):
                if k == reach and (i < pieces // 2) != (way == 0):
                    continue
                rel = -k if way == 0 else k
                ref = piece(lax.rem(zpeer(rel), n_chunks), i)
                remote(ref, ref, psend.at[way], prsem.at[way, k, i], partner).wait_recv()
                if k < reach:
                    pass_on(way, rel, k + 1, i)

    arrived(PX.at[pl.ds(0, ne - 1)], pxsem)
    mine_p = lax.rem(t, n_chunks)
    for a in (0, 1):
        XP[mine_p, :, a * LANES : (a + 1) * LANES] = PX[:, a * cap : (a + 1) * cap, :].reshape(slots, LANES)
    for i in range(pieces):
        for way in (0, 1):
            pass_on(way, 0, 1, i)
    GB[...] = PX[:, 2 * cap :, :].reshape(slots, LANES).astype(F32)
    ACC[...] = jnp.zeros_like(ACC)
    route_q(1)

    do(work, 2)
    for k in range(1, reach):
        ring_p(k)
        do(work, -(-len(work) // (reach - k)))
        if k == reach - 1:
            do(chunks, 2 * reach - 3)
        elif k > 1:
            do(chunks, 2)
    do(work, len(work))
    parts_q(0)
    dot_q(0)
    ring_p(reach)
    do(chunks, len(chunks))
    parts_q(1)
    remote(SPART.at[other], SPX, spsem.at[0], spsem.at[1], partner).start()
    dot_q(1)

    weighed = ACC[:, 0:LANES] * HS[:, 0:LANES].astype(F32)
    for c in range(LANES, units, LANES):
        weighed += ACC[:, c : c + LANES] * HS[:, c : c + LANES].astype(F32)
    weighed = jnp.sum(weighed, axis=1, keepdims=True)
    at_place = jnp.bitwise_and(iota((slots, LANES), 0), cap - 1) == iota((slots, LANES), 1)
    GM[...] = jnp.sum(
        jnp.where(at_place, weighed, 0.0).reshape(ne, cap, LANES), axis=1, keepdims=True
    )
    for o in range(1, ne):
        remote(GM.at[xpeer(o)], GV.at[e], gxsem.at[0], gxsem.at[1], at_x(o)).start()
    GV[e] = GM[e]

    arrived(SPX, spsem)
    SSUM[...] = SPART[d] + SPX[...]
    for k in range(1, nt):
        remote(SSUM, SRECV.at[t], srsem.at[0], srsem.at[1], at_z(k)).start()
    SRECV[t] = SSUM[...]

    for c in range(0, units, LANES):
        HG[:, c : c + LANES] = (ACC[:, c : c + LANES] * GB[...]).astype(BF16)
    save = pltpu.make_async_copy(HG, hg_out, lsem.at[0])
    save.start()

    arrived(GV.at[pl.ds(0, ne - 1)], gxsem)
    values = jnp.concatenate([GV[i] for i in range(ne)], axis=0)
    place_row = iota((LANES, group), 0).astype(F32)
    pair_rows = []
    for k in (0, 1):
        chosen = jnp.where(place_row == place[k][:, 2 * group :], 1.0, 0.0)
        spread = jnp.dot(values, chosen, precision=lax.Precision.HIGHEST, preferred_element_type=F32)
        pair_rows.append(jnp.sum(spread * names[k][:, 2 * group :], axis=0, keepdims=True))
    PV[...] = jnp.concatenate(pair_rows, axis=0)
    for k in range(1, nt):
        remote(PV, PVR.at[t], gzsem.at[0], gzsem.at[1], at_z(k)).start()
    PVR[t] = PV[...]

    arrived(SRECV.at[pl.ds(0, nt - 1)], srsem)
    total = SRECV[0]
    for i in range(1, nt):
        total += SRECV[i]
    for i in range(blocks):
        sg_out[:, i * LANES : (i + 1) * LANES] = total[i]

    arrived(PVR.at[pl.ds(0, nt - 1)], gzsem)
    total = PVR[0]
    for i in range(1, nt):
        total += PVR[i]
    mine = jnp.where(iota((group, 8), 0) == t * 8 + iota((group, 8), 1), 1.0, 0.0)
    gg_out[...] = jnp.dot(total, mine, precision=lax.Precision.HIGHEST, preferred_element_type=F32)

    left_here(TOKP.at[pl.ds(0, nt - 1)], zsem)
    left_here(S.at[d], ssem)
    left_here(dw, wsem)
    left_here(PMSG.at[pl.ds(0, ne - 1)], pxsem)
    for i in (0, 1):
        left_here(QT.at[i, pl.ds(0, nt - 1)], qbsem.at[i])
        left_here(QS.at[i, pl.ds(0, ne - 1)], xqsem.at[i])
    for way in (0, 1):
        ref = XP.at[pl.ds(0, 2 * reach - 1), pl.ds(0, slots // 2)]
        remote(ref, ref, psend.at[way], prsem.at[way, 1, 0], partner).wait_send()
    left_here(GM.at[pl.ds(0, ne - 1)], gxsem)
    left_here(PVR.at[pl.ds(0, nt - 1)], gzsem)
    left_here(SPX, spsem)
    left_here(SRECV.at[pl.ds(0, nt - 1)], srsem)
    save.wait()


def write_kernel(hg, sg, gg, hg_out, sg_out, gg_out):
    hg_out[...] = hg[...]
    sg_out[...] = sg[...]
    gg_out[...] = gg[...]


def on_device(nt, ne, out_grad, routing, gate_codes, hidden_saved, down_weight, channel_scale):
    cap = hidden_saved.shape[3]
    units = hidden_saved.shape[4]
    half = down_weight.shape[2]
    group = routing.shape[0]
    slots = ne * cap
    n_chunks = nt // 2
    qhalf = half - n_chunks * LANES
    blocks = half // LANES
    vmem = pl.BlockSpec(memory_space=pltpu.VMEM)
    anywhere = pl.BlockSpec(memory_space=pl.ANY)
    dma = pltpu.SemaphoreType.DMA
    results = (
        jax.ShapeDtypeStruct((slots, units), BF16),
        jax.ShapeDtypeStruct((1, half), F32),
        jax.ShapeDtypeStruct((2, 8), F32),
    )
    parts = pl.pallas_call(
        functools.partial(kernel, nt, ne, cap, units, half),
        out_shape=results,
        in_specs=[vmem, vmem, vmem, vmem, anywhere, anywhere],
        out_specs=(anywhere, vmem, vmem),
        scratch_shapes=[
            pltpu.VMEM((2, units, half), BF16),
            pltpu.VMEM((2, 8, half), F32),
            pltpu.VMEM((slots, units), BF16),
            pltpu.VMEM((2, units, half), BF16),
            pltpu.VMEM((units, 256), BF16),
            pltpu.VMEM((2, slots, half), F32),
            pltpu.VMEM((nt, 16, LANES), BF16),
            pltpu.VMEM((n_chunks, 16, LANES), BF16),
            pltpu.VMEM((2, nt, 16, qhalf // 2), BF16),
            pltpu.VMEM((ne, 3 * cap, LANES), BF16),
            pltpu.VMEM((ne, 3 * cap, LANES), BF16),
            pltpu.VMEM((n_chunks, slots, 2 * LANES), BF16),
            pltpu.VMEM((2, ne, cap, qhalf), BF16),
            pltpu.VMEM((2, ne, cap, qhalf), BF16),
            pltpu.VMEM((slots, units), F32),
            pltpu.VMEM((slots, LANES), F32),
            pltpu.VMEM((slots, units), BF16),
            pltpu.VMEM((2, blocks, 1, LANES), F32),
            pltpu.VMEM((blocks, 1, LANES), F32),
            pltpu.VMEM((blocks, 1, LANES), F32),
            pltpu.VMEM((nt, blocks, 1, LANES), F32),
            pltpu.VMEM((ne, 1, LANES), F32),
            pltpu.VMEM((ne, 1, LANES), F32),
            pltpu.VMEM((2, group), F32),
            pltpu.VMEM((nt, 2, group), F32),
            dma((2,)),
            dma((2,)),
            dma((2,)),
            dma((2,)),
            dma((2, 3)),
            dma((2, 2)),
            dma((2,)),
            dma((2, n_chunks // 2 + 1, 4)),
            dma((2,)),
            dma((2, 2)),
            dma((2,)),
            dma((2,)),
            dma((2,)),
            dma((2,)),
        ],
        compiler_params=pltpu.CompilerParams(
            collective_id=0, has_side_effects=True, vmem_limit_bytes=60 * 1024 * 1024
        ),
    )(
        out_grad,
        routing.T,
        gate_codes.T,
        channel_scale,
        hidden_saved.reshape(slots, units),
        down_weight.reshape(units, half),
    )
    steps = 4
    tall = pl.BlockSpec((slots // steps, units), lambda i: (i, 0))
    flat = pl.BlockSpec((1, half), lambda i: (0, 0))
    pairs = pl.BlockSpec((2, 8), lambda i: (0, 0))
    hidden_grad, scale_grad, gate_grad = pl.pallas_call(
        write_kernel,
        out_shape=results,
        grid=(steps,),
        in_specs=[tall, flat, pairs],
        out_specs=(tall, flat, pairs),
    )(*parts)
    return hidden_grad.reshape(hidden_saved.shape), scale_grad, gate_grad.T


def solution(mesh):
    in_specs = (
        P(("dp", "expert", "tensor"), None),
        P(("dp", "expert"), None),
        P(("dp", "expert"), None),
        P("dp", "expert", None, None, "tensor"),
        P("expert", "tensor", "dp"),
        P("expert", "dp"),
    )
    out_specs = (
        P("dp", "expert", None, None, "tensor"),
        P("expert", "dp"),
        P(("dp", "expert", "tensor"), None),
    )
    return jax.shard_map(
        functools.partial(on_device, mesh.shape["tensor"], mesh.shape["expert"]),
        mesh=mesh,
        in_specs=in_specs,
        out_specs=out_specs,
        check_vma=False,
    )
```

time: 105 us -> 82.9 us (0.79)
  Pallas kernels: 95.3 us -> 81.7 us
  local copies, waits for them, and re-layouts: 7.5 us -> 0 us
    pallas_call x1, Pallas kernels: 95.3 us -> 78.4 us  [on_device(): pl.pallas_call(functools.partial(kernel, nt, ne, cap, units, half), out_s...]
    unnamed x5 -> x0, local copies, waits for them, and re-layouts: 7.5 us -> none
    pallas_call x0 -> x1, Pallas kernels: none -> 3.28 us  [on_device(): pl.pallas_call(write_kernel, out_shape=results, grid=(steps,), in_specs=[...]
where the time goes in v2:
time: 82.9 us; the launch traced here: 82.3 us
  Pallas kernels  81.7 us (99%)
    pallas_call x1, Pallas kernels, on_device(): pl.pallas_call(functools.partial(kernel, nt, ne, cap, units, half), out_s...  78.4 us
    pallas_call x1, Pallas kernels, on_device(): pl.pallas_call(write_kernel, out_shape=results, grid=(steps,), in_specs=[...  3.28 us

profile of v2, /device:TPU:6, one launch (start us, length us, event | category | flops | bytes accessed | tf_op | source)
XLA Modules:
  0.0 82.3 jit_solution(9322980457804805432)
XLA Ops:
  0.6 78.4 %shard_map.85 = (bf16[512,768]{1,0:T(8,128)(2,1)}, f32[1,2048]{1,0:T(1,128)}, f32[2,8]{1,0:T(2,128)}) custom-call(bf16[8,4096]{1,0:T(8,128)(2,1)} %og.1, s32[2,128]{1,0:T(2,128)} %bitcast.8, s32[2,128]{1,0:T(2,128)} %bitcast.9, bf16[1,2048]{1,0:T(2,128)(2,1)} %cs.1, bf16[512,768]{1,0:T(8,128)(2,1)} %bitcast.7, bf16[768,2048]{1,0:T(8,128)(2,1)} %bitcast.6), custom_call_target="tpu_custom_call" | custom-call | tf_op jit(solution)/shard_map/pallas_call | solution.py:421
  79.1 3.3 %shard_map.86 = (bf16[512,768]{1,0:T(8,128)(2,1)}, f32[1,2048]{1,0:T(1,128)}, f32[2,8]{1,0:T(2,128)}) custom-call(bf16[512,768]{1,0:T(8,128)(2,1)} %get-tuple-element.9.hg, f32[1,2048]{1,0:T(1,128)} %get-tuple-element.10.sg, f32[2,8]{1,0:T(2,128)} %get-tuple-element.11.gg), custom_call_target="tpu_custom_call" | custom-call | tf_op jit(solution)/shard_map/pallas_call | solution.py:482

commit v3 on v2

--- a/solution.py
+++ b/solution.py
@@ -37,9 +37,9 @@
 
 def kernel(
     nt, ne, cap, units, half,
-    og, rt, gc, cs, hs, dw,
+    og_in, rt_in, gc_in, cs_in, hs, dw,
     hg_out, sg_out, gg_out,
-    W, S, HS, QZ, SL, TM, TOKP, SRCP, QT, PMSG, PX, XP, QS, XQ, ACC, GB, HG,
+    og, rt, gc, cs, W, S, HS, QZ, SL, TM, TOKP, SRCP, QT, PMSG, PX, XP, QS, XQ, ACC, GB, HG,
     SPART, SPX, SSUM, SRECV, GM, GV, PV, PVR,
     lsem, wsem, ssem, zsem, qasem, qbsem, pxsem, prsem, psend, xqsem,
     gxsem, gzsem, spsem, srsem,
@@ -82,17 +82,19 @@
     def left_here(ref, sems):
         remote(ref, ref, sems.at[0], sems.at[1], partner).wait_send()
 
-    load_w = pltpu.make_async_copy(dw, W.at[d], lsem.at[0])
-    load_h = pltpu.make_async_copy(hs, HS, lsem.at[1])
-    load_w.start()
-    load_h.start()
-
     barrier = pltpu.get_barrier_semaphore()
-    for k in range(1, nt):
+    for k in sorted(range(1, nt), key=lambda k: -min(k, nt - k)):
         pl.semaphore_signal(barrier, inc=1, device_id=at_z(k), device_id_type=MESH)
-    for o in range(1, ne):
+    for o in range(ne - 1, 0, -1):
         pl.semaphore_signal(barrier, inc=1, device_id=at_x(o), device_id_type=MESH)
     pl.semaphore_signal(barrier, inc=1, device_id=partner, device_id_type=MESH)
+
+    pairs = ((og_in, og), (cs_in, cs), (rt_in, rt), (gc_in, gc), (dw, W.at[d]), (hs, HS))
+    loads = [pltpu.make_async_copy(a, b, lsem.at[i]) for i, (a, b) in enumerate(pairs)]
+    for load in loads:
+        load.start()
+    for load in loads[:4]:
+        load.wait()
 
     def two_rows(first, second, width):
         upper = og[:, first : first + width].astype(F32)
@@ -124,11 +126,10 @@
         remote(chunk, chunk, qbsem.at[i, 0], qasem.at[i, via.index(rel)], partner).wait_recv()
         send_tokens(i, rel, plan[rel])
 
-    send_tokens(0, 0, plan[0][:3])
     for k in range(1, nt):
         source = SRCP.at[lax.rem(zpeer(k), n_chunks)]
         remote(source, TOKP.at[t], zsem.at[0], zsem.at[1], at_z(k)).start()
-    send_tokens(0, 0, plan[0][3:])
+    send_tokens(0, 0, plan[0])
     send_tokens(1, 0, plan[0])
     remote(S.at[d], S.at[d], ssem.at[0], ssem.at[1], partner).start()
     remote(dw, W.at[d], wsem.at[0], wsem.at[1], partner).start()
@@ -164,8 +165,8 @@
     gates = jnp.dot(gate_pick, jnp.ones((group, LANES), BF16), preferred_element_type=F32)
     PMSG[:, 2 * cap :, :] = (gates * (1.0 / 256.0)).astype(BF16).reshape(ne, cap, LANES)
 
-    load_w.wait()
-    load_h.wait()
+    for load in loads[4:]:
+        load.wait()
 
     def unit(hh, block):
         lanes = slice(block * 256, block * 256 + 256)
@@ -180,7 +181,7 @@
             SL[at, :] = (b - u * (1.0 - b * b)).astype(BF16)
             return carry
 
-        lax.fori_loop(0, units // 128, rows, 0)
+        lax.fori_loop(0, units // 128, rows, 0, unroll=True)
         TM[hh, :, lanes] = jnp.dot(HS[...], SL[...], preferred_element_type=F32)
 
     def partner_ready():
@@ -206,7 +207,6 @@
         )
 
     def parts_q(i):
-        arrived(XQ.at[i, pl.ds(0, ne - 1)], xqsem.at[i])
         for a in (0, 1):
             for c in range(part // LANES):
                 at = i * part + c * LANES
@@ -239,7 +239,7 @@
                 jobs.pop(0)()
 
 
-    do(work, 2)
+    do(work, pb)
     for rel in via[:2]:
         tokens_from(0, rel)
 
@@ -256,7 +256,7 @@
         tokens_from(0, rel)
     for rel in via:
         tokens_from(1, rel)
-    do(work, 2)
+    do(work, 1 + pb)
 
     n_direct = nt - 1 - len(via)
 
@@ -275,9 +275,7 @@
             remote(QS.at[i, xpeer(o)], XQ.at[i, e], xqsem.at[i, 0], xqsem.at[i, 1], at_x(o)).start()
         XQ[i, e] = QS[i, e]
 
-    route_q(0)
-
-    pieces = 4
+    pieces = 8
     prow = slots // pieces
 
     def piece(j, i):
@@ -307,25 +305,23 @@
     for i in range(pieces):
         for way in (0, 1):
             pass_on(way, 0, 1, i)
+    route_q(0)
     GB[...] = PX[:, 2 * cap :, :].reshape(slots, LANES).astype(F32)
     ACC[...] = jnp.zeros_like(ACC)
     route_q(1)
 
-    do(work, 2)
+    do(work, qb)
     for k in range(1, reach):
         ring_p(k)
-        do(work, -(-len(work) // (reach - k)))
-        if k == reach - 1:
-            do(chunks, 2 * reach - 3)
-        elif k > 1:
-            do(chunks, 2)
+        do(work, len(work))
+        do(chunks, 3 if k == 1 else 2)
     do(work, len(work))
+    arrived(XQ.at[0, pl.ds(0, ne - 1)], xqsem.at[0])
     parts_q(0)
     dot_q(0)
     ring_p(reach)
     do(chunks, len(chunks))
-    parts_q(1)
-    remote(SPART.at[other], SPX, spsem.at[0], spsem.at[1], partner).start()
+    arrived(XQ.at[1, pl.ds(0, ne - 1)], xqsem.at[1])
     dot_q(1)
 
     weighed = ACC[:, 0:LANES] * HS[:, 0:LANES].astype(F32)
@@ -340,6 +336,8 @@
         remote(GM.at[xpeer(o)], GV.at[e], gxsem.at[0], gxsem.at[1], at_x(o)).start()
     GV[e] = GM[e]
 
+    parts_q(1)
+    remote(SPART.at[other], SPX, spsem.at[0], spsem.at[1], partner).start()
     arrived(SPX, spsem)
     SSUM[...] = SPART[d] + SPX[...]
     for k in range(1, nt):
@@ -421,9 +419,13 @@
     parts = pl.pallas_call(
         functools.partial(kernel, nt, ne, cap, units, half),
         out_shape=results,
-        in_specs=[vmem, vmem, vmem, vmem, anywhere, anywhere],
+        in_specs=[anywhere] * 6,
         out_specs=(anywhere, vmem, vmem),
         scratch_shapes=[
+            pltpu.VMEM(out_grad.shape, BF16),
+            pltpu.VMEM((2, group), jnp.int32),
+            pltpu.VMEM((2, group), jnp.int32),
+            pltpu.VMEM((1, half), BF16),
             pltpu.VMEM((2, units, half), BF16),
             pltpu.VMEM((2, 8, half), F32),
             pltpu.VMEM((slots, units), BF16),
@@ -449,14 +451,14 @@
             pltpu.VMEM((ne, 1, LANES), F32),
             pltpu.VMEM((2, group), F32),
             pltpu.VMEM((nt, 2, group), F32),
-            dma((2,)),
+            dma((6,)),
             dma((2,)),
             dma((2,)),
             dma((2,)),
             dma((2, 3)),
             dma((2, 2)),
             dma((2,)),
-            dma((2, n_chunks // 2 + 1, 4)),
+            dma((2, n_chunks // 2 + 1, 8)),
             dma((2,)),
             dma((2, 2)),
             dma((2,)),
@@ -475,16 +477,11 @@
         hidden_saved.reshape(slots, units),
         down_weight.reshape(units, half),
     )
-    steps = 4
-    tall = pl.BlockSpec((slots // steps, units), lambda i: (i, 0))
-    flat = pl.BlockSpec((1, half), lambda i: (0, 0))
-    pairs = pl.BlockSpec((2, 8), lambda i: (0, 0))
     hidden_grad, scale_grad, gate_grad = pl.pallas_call(
         write_kernel,
         out_shape=results,
-        grid=(steps,),
-        in_specs=[tall, flat, pairs],
-        out_specs=(tall, flat, pairs),
+        in_specs=[vmem] * 3,
+        out_specs=(vmem,) * 3,
     )(*parts)
     return hidden_grad.reshape(hidden_saved.shape), scale_grad, gate_grad.T
 

time: 82.9 us -> 75.7 us (0.913); the launches traced: 82.3 us -> 74.3 us
  Pallas kernels: 81.7 us -> 73.7 us
    pallas_call x1, Pallas kernels: 78.4 us -> 71.6 us  [on_device(): pl.pallas_call(functools.partial(kernel, nt, ne, cap, units, half), out_s...]
    pallas_call x1, Pallas kernels: 3.28 us -> 2.09 us  [on_device(): pl.pallas_call(write_kernel, out_shape=results, in_specs=[vmem] * 3, out_...]
where the time goes in v3:
time: 75.7 us; the launch traced here: 74.3 us
  Pallas kernels  73.7 us (97%)
    pallas_call x1, Pallas kernels, on_device(): pl.pallas_call(functools.partial(kernel, nt, ne, cap, units, half), out_s...  71.6 us
    pallas_call x1, Pallas kernels, on_device(): pl.pallas_call(write_kernel, out_shape=results, in_specs=[vmem] * 3, out_...  2.09 us

profile of v3, /device:TPU:6, one launch (start us, length us, event | category | flops | bytes accessed | tf_op | source)
XLA Modules:
  0.0 74.3 jit_solution(3500872970532009947)
XLA Ops:
  0.6 71.6 %shard_map.85 = (bf16[512,768]{1,0:T(8,128)(2,1)}, f32[1,2048]{1,0:T(1,128)}, f32[2,8]{1,0:T(2,128)}) custom-call(bf16[8,4096]{1,0:T(8,128)(2,1)} %og_in.1, s32[2,128]{1,0:T(2,128)} %bitcast.8, s32[2,128]{1,0:T(2,128)} %bitcast.9, bf16[1,2048]{1,0:T(2,128)(2,1)} %cs_in.1, bf16[512,768]{1,0:T(8,128)(2,1)} %bitcast.7, bf16[768,2048]{1,0:T(8,128)(2,1)} %bitcast.6), custom_call_target="tpu_custom_call" | custom-call | tf_op jit(solution)/shard_map/pallas_call | solution.py:419
  72.2 2.1 %shard_map.86 = (bf16[512,768]{1,0:T(8,128)(2,1)}, f32[1,2048]{1,0:T(1,128)}, f32[2,8]{1,0:T(2,128)}) custom-call(bf16[512,768]{1,0:T(8,128)(2,1)} %get-tuple-element.9.hg, f32[1,2048]{1,0:T(1,128)} %get-tuple-element.10.sg, f32[2,8]{1,0:T(2,128)} %get-tuple-element.11.gg), custom_call_target="tpu_custom_call" | custom-call | tf_op jit(solution)/shard_map/pallas_call | solution.py:480

commit v4 on v3

--- a/solution.py
+++ b/solution.py
@@ -29,10 +29,24 @@
     return lax.broadcasted_iota(jnp.int32, shape, axis)
 
 
-def gather_plan(nt):
-    if nt == 16:
+def three_parts(x):
+    first = x.astype(BF16)
+    rest = x - first.astype(F32)
+    second = rest.astype(BF16)
+    third = (rest - second.astype(F32)).astype(BF16)
+    return jnp.concatenate([first, second, third], axis=0)
+
+
+def part_widths(qhalf):
+    if qhalf == 8 * LANES:
+        return (2 * LANES, 3 * LANES, 3 * LANES)
+    return (LANES,) * (qhalf // LANES)
+
+
+def gather_plan(nt, i):
+    if nt == 16 and i > 0:
         return {0: (8, 4, -4, 1, -1, 2, -2), -4: (1, -1, 2), 4: (1, -1, -2), 8: (1, -1)}
-    return {0: tuple(range(1, nt))}
+    return {0: tuple(sorted(range(1, nt), key=lambda k: -min(k, nt - k)))}
 
 
 def kernel(
@@ -40,7 +54,7 @@
     og_in, rt_in, gc_in, cs_in, hs, dw,
     hg_out, sg_out, gg_out,
     og, rt, gc, cs, W, S, HS, QZ, SL, TM, TOKP, SRCP, QT, PMSG, PX, XP, QS, XQ, ACC, GB, HG,
-    SPART, SPX, SSUM, SRECV, GM, GV, PV, PVR,
+    SPART, SPX, SSUM, SRECV, GM, GV, PV, PVR, CH, NM,
     lsem, wsem, ssem, zsem, qasem, qbsem, pxsem, prsem, psend, xqsem,
     gxsem, gzsem, spsem, srsem,
 ):
@@ -56,7 +70,9 @@
     per_half = n_chunks // 2
     phalf = per_half * chunk_w
     qhalf = half - phalf
-    part = qhalf // 2
+    widths = part_widths(qhalf)
+    offsets = [phalf + sum(widths[:i]) for i in range(len(widths))]
+    last = len(widths) - 1
     blocks = half // LANES
     reach = n_chunks // 2
     other = 1 - d
@@ -101,8 +117,8 @@
         lower = og[:, second : second + width].astype(F32)
         return jnp.concatenate([upper, lower], axis=0).astype(BF16)
 
-    for i in (0, 1):
-        QT[i, t] = two_rows(phalf + i * part, half + phalf + i * part, part)
+    for i, width in enumerate(widths):
+        QT[i][t] = two_rows(offsets[i], half + offsets[i], width)
     for j in range(n_chunks):
         start = (j // per_half) * half + (j % per_half) * chunk_w
         SRCP[j] = two_rows(start, start + LANES, LANES)
@@ -111,26 +127,29 @@
 
     pl.semaphore_wait(barrier, nt + ne - 1)
 
-    plan = gather_plan(nt)
-    via = [rel for rel in plan if rel]
-
-    def send_tokens(i, rel, offsets):
-        chunk = QT.at[i, zpeer(rel)]
-        for k in offsets:
+    plans = [gather_plan(nt, i) for i in range(len(widths))]
+    vias = [[rel for rel in plan if rel] for plan in plans]
+
+    def send_tokens(i, rel):
+        chunk = QT[i].at[zpeer(rel)]
+        for k in plans[i][rel]:
             seen = -k if k != 8 else 8
-            recv = qasem.at[i, via.index(seen)] if rel == 0 and seen in via else qbsem.at[i, 1]
+            known = rel == 0 and seen in vias[i]
+            recv = qasem.at[i, vias[i].index(seen)] if known else qbsem.at[i, 1]
             remote(chunk, chunk, qbsem.at[i, 0], recv, at_z(k)).start()
 
-    def tokens_from(i, rel):
-        chunk = QT.at[i, zpeer(rel)]
-        remote(chunk, chunk, qbsem.at[i, 0], qasem.at[i, via.index(rel)], partner).wait_recv()
-        send_tokens(i, rel, plan[rel])
+    def tokens_from(i, rels):
+        for rel in rels:
+            chunk = QT[i].at[zpeer(rel)]
+            sem = qasem.at[i, vias[i].index(rel)]
+            remote(chunk, chunk, qbsem.at[i, 0], sem, partner).wait_recv()
+            send_tokens(i, rel)
 
     for k in range(1, nt):
         source = SRCP.at[lax.rem(zpeer(k), n_chunks)]
         remote(source, TOKP.at[t], zsem.at[0], zsem.at[1], at_z(k)).start()
-    send_tokens(0, 0, plan[0])
-    send_tokens(1, 0, plan[0])
+    for i in range(len(widths)):
+        send_tokens(i, 0)
     remote(S.at[d], S.at[d], ssem.at[0], ssem.at[1], partner).start()
     remote(dw, W.at[d], wsem.at[0], wsem.at[1], partner).start()
 
@@ -165,6 +184,11 @@
     gates = jnp.dot(gate_pick, jnp.ones((group, LANES), BF16), preferred_element_type=F32)
     PMSG[:, 2 * cap :, :] = (gates * (1.0 / 256.0)).astype(BF16).reshape(ne, cap, LANES)
 
+    place_row = iota((LANES, group), 0).astype(F32)
+    for k in (0, 1):
+        at = slice(k * group, (k + 1) * group)
+        CH[:, at] = jnp.where(place_row == place[k][:, 2 * group :], 1.0, 0.0).astype(BF16)
+        NM[:, at] = names[k][:, 2 * group :]
     for load in loads[4:]:
         load.wait()
 
@@ -207,20 +231,24 @@
         )
 
     def parts_q(i):
+        width = widths[i]
         for a in (0, 1):
-            for c in range(part // LANES):
-                at = i * part + c * LANES
-                x = XQ[i, :, :, a * part + c * LANES : a * part + (c + 1) * LANES]
-                SPART[a, (phalf + at) // LANES] = terms(x.reshape(slots, LANES), a, phalf + at)
+            for c in range(width // LANES):
+                at = offsets[i] + c * LANES
+                x = XQ[i][:, :, a * width + c * LANES : a * width + (c + 1) * LANES]
+                SPART[a, at // LANES] = terms(x.reshape(slots, LANES), a, at)
 
     def dot_q(i):
-        for a in (0, 1):
-            ACC[...] += lax.dot_general(
-                XQ[i, :, :, a * part : (a + 1) * part].reshape(slots, part),
-                QZ[a, :, phalf + i * part : phalf + (i + 1) * part],
-                (((1,), (1,)), ((), ())),
-                preferred_element_type=F32,
-            )
+        lanes = slice(offsets[i], offsets[i] + widths[i])
+        ACC[...] += lax.dot_general(
+            XQ[i][...].reshape(slots, 2 * widths[i]),
+            jnp.concatenate([QZ[0, :, lanes], QZ[1, :, lanes]], axis=1),
+            (((1,), (1,)), ((), ())),
+            preferred_element_type=F32,
+        )
+
+    def arrived_q(i):
+        arrived(XQ[i].at[pl.ds(0, ne - 1)], xqsem.at[i])
 
     pb, qb = phalf // 256, qhalf // 256
     work = [functools.partial(unit, d, b) for b in range(pb)]
@@ -240,8 +268,6 @@
 
 
     do(work, pb)
-    for rel in via[:2]:
-        tokens_from(0, rel)
 
     arrived(TOKP.at[pl.ds(0, nt - 1)], zsem)
     tokens = TOKP[...].reshape(2 * group, LANES)
@@ -252,28 +278,28 @@
         remote(PMSG.at[xpeer(o)], PX.at[e], pxsem.at[0], pxsem.at[1], at_x(o)).start()
     PX[e] = PMSG[e]
 
-    for rel in via[2:]:
-        tokens_from(0, rel)
-    for rel in via:
-        tokens_from(1, rel)
+    def route_q(i):
+        width = widths[i]
+        arrived(QT[i].at[pl.ds(0, nt - 1 - len(vias[i]))], qbsem.at[i])
+        gathered = QT[i][...].reshape(2 * group, width)
+        for a in (0, 1):
+            QS[i][:, :, a * width : (a + 1) * width] = (
+                jnp.dot(pick_q[a], gathered, preferred_element_type=F32)
+                .astype(BF16)
+                .reshape(ne, cap, width)
+            )
+        for o in range(1, ne):
+            source, target = QS[i].at[xpeer(o)], XQ[i].at[e]
+            remote(source, target, xqsem.at[i, 0], xqsem.at[i, 1], at_x(o)).start()
+        XQ[i][e] = QS[i][e]
+
+    for i in range(1, len(widths)):
+        tokens_from(i, vias[i][:2])
+        if i == 1:
+            route_q(0)
+    for i in range(1, len(widths)):
+        tokens_from(i, vias[i][2:])
     do(work, 1 + pb)
-
-    n_direct = nt - 1 - len(via)
-
-    def route_q(i):
-        arrived(QT.at[i, pl.ds(0, n_direct)], qbsem.at[i])
-        gathered = QT[i].reshape(2 * group, part)
-        step = min(256, part)
-        for a in (0, 1):
-            for c in range(0, part, step):
-                QS[i, :, :, a * part + c : a * part + c + step] = (
-                    jnp.dot(pick_q[a], gathered[:, c : c + step], preferred_element_type=F32)
-                    .astype(BF16)
-                    .reshape(ne, cap, step)
-                )
-        for o in range(1, ne):
-            remote(QS.at[i, xpeer(o)], XQ.at[i, e], xqsem.at[i, 0], xqsem.at[i, 1], at_x(o)).start()
-        XQ[i, e] = QS[i, e]
 
     pieces = 8
     prow = slots // pieces
@@ -305,10 +331,11 @@
     for i in range(pieces):
         for way in (0, 1):
             pass_on(way, 0, 1, i)
-    route_q(0)
+    route_q(1)
     GB[...] = PX[:, 2 * cap :, :].reshape(slots, LANES).astype(F32)
     ACC[...] = jnp.zeros_like(ACC)
-    route_q(1)
+    for i in range(2, len(widths)):
+        route_q(i)
 
     do(work, qb)
     for k in range(1, reach):
@@ -316,13 +343,14 @@
         do(work, len(work))
         do(chunks, 3 if k == 1 else 2)
     do(work, len(work))
-    arrived(XQ.at[0, pl.ds(0, ne - 1)], xqsem.at[0])
-    parts_q(0)
-    dot_q(0)
+    for i in range(last):
+        arrived_q(i)
+        parts_q(i)
+        dot_q(i)
     ring_p(reach)
     do(chunks, len(chunks))
-    arrived(XQ.at[1, pl.ds(0, ne - 1)], xqsem.at[1])
-    dot_q(1)
+    arrived_q(last)
+    dot_q(last)
 
     weighed = ACC[:, 0:LANES] * HS[:, 0:LANES].astype(F32)
     for c in range(LANES, units, LANES):
@@ -336,7 +364,7 @@
         remote(GM.at[xpeer(o)], GV.at[e], gxsem.at[0], gxsem.at[1], at_x(o)).start()
     GV[e] = GM[e]
 
-    parts_q(1)
+    parts_q(last)
     remote(SPART.at[other], SPX, spsem.at[0], spsem.at[1], partner).start()
     arrived(SPX, spsem)
     SSUM[...] = SPART[d] + SPX[...]
@@ -351,12 +379,10 @@
 
     arrived(GV.at[pl.ds(0, ne - 1)], gxsem)
     values = jnp.concatenate([GV[i] for i in range(ne)], axis=0)
-    place_row = iota((LANES, group), 0).astype(F32)
-    pair_rows = []
-    for k in (0, 1):
-        chosen = jnp.where(place_row == place[k][:, 2 * group :], 1.0, 0.0)
-        spread = jnp.dot(values, chosen, precision=lax.Precision.HIGHEST, preferred_element_type=F32)
-        pair_rows.append(jnp.sum(spread * names[k][:, 2 * group :], axis=0, keepdims=True))
+    spread = jnp.dot(three_parts(values), CH[...], preferred_element_type=F32)
+    spread = (spread[:ne] + spread[ne : 2 * ne] + spread[2 * ne :]) * NM[...]
+    pair_row = jnp.sum(spread, axis=0, keepdims=True)
+    pair_rows = [pair_row[:, :group], pair_row[:, group:]]
     PV[...] = jnp.concatenate(pair_rows, axis=0)
     for k in range(1, nt):
         remote(PV, PVR.at[t], gzsem.at[0], gzsem.at[1], at_z(k)).start()
@@ -373,16 +399,17 @@
     total = PVR[0]
     for i in range(1, nt):
         total += PVR[i]
-    mine = jnp.where(iota((group, 8), 0) == t * 8 + iota((group, 8), 1), 1.0, 0.0)
-    gg_out[...] = jnp.dot(total, mine, precision=lax.Precision.HIGHEST, preferred_element_type=F32)
+    mine = jnp.where(iota((group, 8), 0) == t * 8 + iota((group, 8), 1), 1.0, 0.0).astype(BF16)
+    picked = jnp.dot(three_parts(total), mine, preferred_element_type=F32)
+    gg_out[...] = picked[0:2] + picked[2:4] + picked[4:6]
 
     left_here(TOKP.at[pl.ds(0, nt - 1)], zsem)
     left_here(S.at[d], ssem)
     left_here(dw, wsem)
     left_here(PMSG.at[pl.ds(0, ne - 1)], pxsem)
-    for i in (0, 1):
-        left_here(QT.at[i, pl.ds(0, nt - 1)], qbsem.at[i])
-        left_here(QS.at[i, pl.ds(0, ne - 1)], xqsem.at[i])
+    for i in range(len(widths)):
+        left_here(QT[i].at[pl.ds(0, nt - 1)], qbsem.at[i])
+        left_here(QS[i].at[pl.ds(0, ne - 1)], xqsem.at[i])
     for way in (0, 1):
         ref = XP.at[pl.ds(0, 2 * reach - 1), pl.ds(0, slots // 2)]
         remote(ref, ref, psend.at[way], prsem.at[way, 1, 0], partner).wait_send()
@@ -406,7 +433,7 @@
     group = routing.shape[0]
     slots = ne * cap
     n_chunks = nt // 2
-    qhalf = half - n_chunks * LANES
+    widths = part_widths(half - n_chunks * LANES)
     blocks = half // LANES
     vmem = pl.BlockSpec(memory_space=pltpu.VMEM)
     anywhere = pl.BlockSpec(memory_space=pl.ANY)
@@ -434,12 +461,12 @@
             pltpu.VMEM((2, slots, half), F32),
             pltpu.VMEM((nt, 16, LANES), BF16),
             pltpu.VMEM((n_chunks, 16, LANES), BF16),
-            pltpu.VMEM((2, nt, 16, qhalf // 2), BF16),
+            [pltpu.VMEM((nt, 16, w), BF16) for w in widths],
             pltpu.VMEM((ne, 3 * cap, LANES), BF16),
             pltpu.VMEM((ne, 3 * cap, LANES), BF16),
             pltpu.VMEM((n_chunks, slots, 2 * LANES), BF16),
-            pltpu.VMEM((2, ne, cap, qhalf), BF16),
-            pltpu.VMEM((2, ne, cap, qhalf), BF16),
+            [pltpu.VMEM((ne, cap, 2 * w), BF16) for w in widths],
+            [pltpu.VMEM((ne, cap, 2 * w), BF16) for w in widths],
             pltpu.VMEM((slots, units), F32),
             pltpu.VMEM((slots, LANES), F32),
             pltpu.VMEM((slots, units), BF16),
@@ -451,16 +478,18 @@
             pltpu.VMEM((ne, 1, LANES), F32),
             pltpu.VMEM((2, group), F32),
             pltpu.VMEM((nt, 2, group), F32),
+            pltpu.VMEM((LANES, 2 * group), BF16),
+            pltpu.VMEM((ne, 2 * group), F32),
             dma((6,)),
             dma((2,)),
             dma((2,)),
             dma((2,)),
-            dma((2, 3)),
-            dma((2, 2)),
+            dma((len(widths), 3)),
+            dma((len(widths), 2)),
             dma((2,)),
             dma((2, n_chunks // 2 + 1, 8)),
             dma((2,)),
-            dma((2, 2)),
+            dma((len(widths), 2)),
             dma((2,)),
             dma((2,)),
             dma((2,)),

time: 75.7 us -> 76.3 us (level)
  no operation moved by 1% of the time
where the time goes in v4:
time: 76.3 us; the launch traced here: 75 us
  Pallas kernels  74.4 us (98%)
    pallas_call x1, Pallas kernels, on_device(): pl.pallas_call(functools.partial(kernel, nt, ne, cap, units, half), out_s...  72.3 us
    pallas_call x1, Pallas kernels, on_device(): pl.pallas_call(write_kernel, out_shape=results, in_specs=[vmem] * 3, out_...  2.09 us

profile of v4, /device:TPU:6, one launch (start us, length us, event | category | flops | bytes accessed | tf_op | source)
XLA Modules:
  0.0 75.0 jit_solution(3754946870662726455)
XLA Ops:
  0.6 72.3 %shard_map.85 = (bf16[512,768]{1,0:T(8,128)(2,1)}, f32[1,2048]{1,0:T(1,128)}, f32[2,8]{1,0:T(2,128)}) custom-call(bf16[8,4096]{1,0:T(8,128)(2,1)} %og_in.1, s32[2,128]{1,0:T(2,128)} %bitcast.8, s32[2,128]{1,0:T(2,128)} %bitcast.9, bf16[1,2048]{1,0:T(2,128)(2,1)} %cs_in.1, bf16[512,768]{1,0:T(8,128)(2,1)} %bitcast.7, bf16[768,2048]{1,0:T(8,128)(2,1)} %bitcast.6), custom_call_target="tpu_custom_call" | custom-call | tf_op jit(solution)/shard_map/pallas_call | solution.py:446
  72.9 2.1 %shard_map.86 = (bf16[512,768]{1,0:T(8,128)(2,1)}, f32[1,2048]{1,0:T(1,128)}, f32[2,8]{1,0:T(2,128)}) custom-call(bf16[512,768]{1,0:T(8,128)(2,1)} %get-tuple-element.9.hg, f32[1,2048]{1,0:T(1,128)} %get-tuple-element.10.sg, f32[2,8]{1,0:T(2,128)} %get-tuple-element.11.gg), custom_call_target="tpu_custom_call" | custom-call | tf_op jit(solution)/shard_map/pallas_call | solution.py:509

commit v5 on v4

--- a/solution.py
+++ b/solution.py
@@ -39,12 +39,12 @@
 
 def part_widths(qhalf):
     if qhalf == 8 * LANES:
-        return (2 * LANES, 3 * LANES, 3 * LANES)
+        return (4 * LANES, 4 * LANES)
     return (LANES,) * (qhalf // LANES)
 
 
-def gather_plan(nt, i):
-    if nt == 16 and i > 0:
+def gather_plan(nt):
+    if nt == 16:
         return {0: (8, 4, -4, 1, -1, 2, -2), -4: (1, -1, 2), 4: (1, -1, -2), 8: (1, -1)}
     return {0: tuple(sorted(range(1, nt), key=lambda k: -min(k, nt - k)))}
 
@@ -127,21 +127,21 @@
 
     pl.semaphore_wait(barrier, nt + ne - 1)
 
-    plans = [gather_plan(nt, i) for i in range(len(widths))]
-    vias = [[rel for rel in plan if rel] for plan in plans]
+    plan = gather_plan(nt)
+    via = [rel for rel in plan if rel]
 
     def send_tokens(i, rel):
         chunk = QT[i].at[zpeer(rel)]
-        for k in plans[i][rel]:
+        for k in plan[rel]:
             seen = -k if k != 8 else 8
-            known = rel == 0 and seen in vias[i]
-            recv = qasem.at[i, vias[i].index(seen)] if known else qbsem.at[i, 1]
+            known = rel == 0 and seen in via
+            recv = qasem.at[i, via.index(seen)] if known else qbsem.at[i, 1]
             remote(chunk, chunk, qbsem.at[i, 0], recv, at_z(k)).start()
 
     def tokens_from(i, rels):
         for rel in rels:
             chunk = QT[i].at[zpeer(rel)]
-            sem = qasem.at[i, vias[i].index(rel)]
+            sem = qasem.at[i, via.index(rel)]
             remote(chunk, chunk, qbsem.at[i, 0], sem, partner).wait_recv()
             send_tokens(i, rel)
 
@@ -238,11 +238,14 @@
                 x = XQ[i][:, :, a * width + c * LANES : a * width + (c + 1) * LANES]
                 SPART[a, at // LANES] = terms(x.reshape(slots, LANES), a, at)
 
-    def dot_q(i):
+    cuts = 1
+
+    def dot_q(i, cut):
         lanes = slice(offsets[i], offsets[i] + widths[i])
-        ACC[...] += lax.dot_general(
+        at = slice(cut * units // cuts, (cut + 1) * units // cuts)
+        ACC[:, at] += lax.dot_general(
             XQ[i][...].reshape(slots, 2 * widths[i]),
-            jnp.concatenate([QZ[0, :, lanes], QZ[1, :, lanes]], axis=1),
+            jnp.concatenate([QZ[0, at, lanes], QZ[1, at, lanes]], axis=1),
             (((1,), (1,)), ((), ())),
             preferred_element_type=F32,
         )
@@ -269,6 +272,8 @@
 
     do(work, pb)
 
+    tokens_from(0, via[:2])
+
     arrived(TOKP.at[pl.ds(0, nt - 1)], zsem)
     tokens = TOKP[...].reshape(2 * group, LANES)
     for a in (0, 1):
@@ -280,7 +285,7 @@
 
     def route_q(i):
         width = widths[i]
-        arrived(QT[i].at[pl.ds(0, nt - 1 - len(vias[i]))], qbsem.at[i])
+        arrived(QT[i].at[pl.ds(0, nt - 1 - len(via))], qbsem.at[i])
         gathered = QT[i][...].reshape(2 * group, width)
         for a in (0, 1):
             QS[i][:, :, a * width : (a + 1) * width] = (
@@ -293,12 +298,9 @@
             remote(source, target, xqsem.at[i, 0], xqsem.at[i, 1], at_x(o)).start()
         XQ[i][e] = QS[i][e]
 
+    tokens_from(0, via[2:])
     for i in range(1, len(widths)):
-        tokens_from(i, vias[i][:2])
-        if i == 1:
-            route_q(0)
-    for i in range(1, len(widths)):
-        tokens_from(i, vias[i][2:])
+        tokens_from(i, via)
     do(work, 1 + pb)
 
     pieces = 8
@@ -313,7 +315,8 @@
         ref = piece(lax.rem(zpeer(rel), n_chunks), i)
         remote(ref, ref, psend.at[way], prsem.at[way, k, i], (right, left)[way]).start()
 
-    def ring_p(k):
+    def ring_p(k, jobs):
+        jobs = list(jobs)
         for i in range(pieces):
             for way in (0, 1):
                 if k == reach and (i < pieces // 2) != (way == 0):
@@ -323,6 +326,8 @@
                 remote(ref, ref, psend.at[way], prsem.at[way, k, i], partner).wait_recv()
                 if k < reach:
                     pass_on(way, rel, k + 1, i)
+            do(jobs, 1)
+        do(jobs, len(jobs))
 
     arrived(PX.at[pl.ds(0, ne - 1)], pxsem)
     mine_p = lax.rem(t, n_chunks)
@@ -331,26 +336,33 @@
     for i in range(pieces):
         for way in (0, 1):
             pass_on(way, 0, 1, i)
-    route_q(1)
+    route_q(0)
     GB[...] = PX[:, 2 * cap :, :].reshape(slots, LANES).astype(F32)
     ACC[...] = jnp.zeros_like(ACC)
-    for i in range(2, len(widths)):
+    for i in range(1, len(widths)):
         route_q(i)
 
-    do(work, qb)
-    for k in range(1, reach):
-        ring_p(k)
-        do(work, len(work))
-        do(chunks, 3 if k == 1 else 2)
-    do(work, len(work))
-    for i in range(last):
-        arrived_q(i)
-        parts_q(i)
-        dot_q(i)
-    ring_p(reach)
-    do(chunks, len(chunks))
+    def idle():
+        pass
+
+    def jobs_q(i):
+        jobs = [functools.partial(arrived_q, i), functools.partial(parts_q, i)]
+        return jobs + [functools.partial(dot_q, i, cut) for cut in range(cuts)]
+
+    pending = [jobs_q(i) for i in range(last)]
+    for k in range(1, reach + 1):
+        jobs = work + [chunks[0]]
+        if k > 1:
+            jobs = [chunks[2 * k - 3], idle, chunks[2 * k - 2], idle]
+        if k == reach - 1:
+            jobs = jobs + pending.pop(0)
+        ring_p(k, jobs)
+    for jobs in pending:
+        do(jobs, len(jobs))
+    do([chunks[-1]], 1)
     arrived_q(last)
-    dot_q(last)
+    for cut in range(cuts):
+        dot_q(last, cut)
 
     weighed = ACC[:, 0:LANES] * HS[:, 0:LANES].astype(F32)
     for c in range(LANES, units, LANES):
@@ -376,6 +388,17 @@
         HG[:, c : c + LANES] = (ACC[:, c : c + LANES] * GB[...]).astype(BF16)
     save = pltpu.make_async_copy(HG, hg_out, lsem.at[0])
     save.start()
+
+    left_here(TOKP.at[pl.ds(0, nt - 1)], zsem)
+    left_here(S.at[d], ssem)
+    left_here(dw, wsem)
+    left_here(PMSG.at[pl.ds(0, ne - 1)], pxsem)
+    for i in range(len(widths)):
+        left_here(QT[i].at[pl.ds(0, nt - 1)], qbsem.at[i])
+        left_here(QS[i].at[pl.ds(0, ne - 1)], xqsem.at[i])
+    for way in (0, 1):
+        ref = XP.at[pl.ds(0, 2 * reach - 1), pl.ds(0, slots // 2)]
+        remote(ref, ref, psend.at[way], prsem.at[way, 1, 0], partner).wait_send()
 
     arrived(GV.at[pl.ds(0, ne - 1)], gxsem)
     values = jnp.concatenate([GV[i] for i in range(ne)], axis=0)
@@ -403,16 +426,6 @@
     picked = jnp.dot(three_parts(total), mine, preferred_element_type=F32)
     gg_out[...] = picked[0:2] + picked[2:4] + picked[4:6]
 
-    left_here(TOKP.at[pl.ds(0, nt - 1)], zsem)
-    left_here(S.at[d], ssem)
-    left_here(dw, wsem)
-    left_here(PMSG.at[pl.ds(0, ne - 1)], pxsem)
-    for i in range(len(widths)):
-        left_here(QT[i].at[pl.ds(0, nt - 1)], qbsem.at[i])
-        left_here(QS[i].at[pl.ds(0, ne - 1)], xqsem.at[i])
-    for way in (0, 1):
-        ref = XP.at[pl.ds(0, 2 * reach - 1), pl.ds(0, slots // 2)]
-        remote(ref, ref, psend.at[way], prsem.at[way, 1, 0], partner).wait_send()
     left_here(GM.at[pl.ds(0, ne - 1)], gxsem)
     left_here(PVR.at[pl.ds(0, nt - 1)], gzsem)
     left_here(SPX, spsem)

time: 76.3 us -> 75.6 us (level)
  Pallas kernels: 74.4 us -> 73.6 us
    pallas_call x1, Pallas kernels: 72.3 us -> 71.5 us  [on_device(): pl.pallas_call(functools.partial(kernel, nt, ne, cap, units, half), out_s...]
where the time goes in v5:
time: 75.6 us; the launch traced here: 74.2 us
  Pallas kernels  73.6 us (97%)
    pallas_call x1, Pallas kernels, on_device(): pl.pallas_call(functools.partial(kernel, nt, ne, cap, units, half), out_s...  71.5 us
    pallas_call x1, Pallas kernels, on_device(): pl.pallas_call(write_kernel, out_shape=results, in_specs=[vmem] * 3, out_...  2.09 us

profile of v5, /device:TPU:6, one launch (start us, length us, event | category | flops | bytes accessed | tf_op | source)
XLA Modules:
  0.0 74.2 jit_solution(14584404021074497641)
XLA Ops:
  0.6 71.5 %shard_map.85 = (bf16[512,768]{1,0:T(8,128)(2,1)}, f32[1,2048]{1,0:T(1,128)}, f32[2,8]{1,0:T(2,128)}) custom-call(bf16[8,4096]{1,0:T(8,128)(2,1)} %og_in.1, s32[2,128]{1,0:T(2,128)} %bitcast.8, s32[2,128]{1,0:T(2,128)} %bitcast.9, bf16[1,2048]{1,0:T(2,128)(2,1)} %cs_in.1, bf16[512,768]{1,0:T(8,128)(2,1)} %bitcast.7, bf16[768,2048]{1,0:T(8,128)(2,1)} %bitcast.6), custom_call_target="tpu_custom_call" | custom-call | tf_op jit(solution)/shard_map/pallas_call | solution.py:459
  72.1 2.1 %shard_map.86 = (bf16[512,768]{1,0:T(8,128)(2,1)}, f32[1,2048]{1,0:T(1,128)}, f32[2,8]{1,0:T(2,128)}) custom-call(bf16[512,768]{1,0:T(8,128)(2,1)} %get-tuple-element.9.hg, f32[1,2048]{1,0:T(1,128)} %get-tuple-element.10.sg, f32[2,8]{1,0:T(2,128)} %get-tuple-element.11.gg), custom_call_target="tpu_custom_call" | custom-call | tf_op jit(solution)/shard_map/pallas_call | solution.py:522
